TPU v7x, 256 devices: a whole 4x4x8 slice. The times are simulated.
256 devices in a mesh: segment: 8 (over z), dp: 32 (over x, y, core).
Axes of the slice: x: 4, y: 4, z: 8, core: 2. Of those that a mesh axis runs over, the one named last changes fastest.
Arguments:
- arriving: float32 [8, 32, 128, 1024], P('segment', 'dp'), may hold values from -6 to 6
- entering: float32 [1, 32, 128, 1024], P(None, 'dp'), may hold values from -6 to 6
- returning: float32 [8, 32, 128, 1024], P('segment', 'dp'), may hold values from -6 to 6
- loss_grad: float32 [1, 32, 128, 1024], P(None, 'dp'), may hold values from -6 to 6
- kept: float32 [8, 3, 32, 128, 1024], P('segment', None, 'dp'), may hold values from -6 to 6
- lent: float32 [8, 3, 32, 128, 1024], P('segment', None, 'dp'), may hold values from -6 to 6
- w_in: float32 [8, 1024, 2048], P('segment', 'dp'), may hold values from -0.1875 to 0.1875
- kernel: float32 [8, 31, 1024], P('segment'), may hold values from -1 to 1
- w_out: float32 [8, 1024, 1024], P('segment', 'dp'), may hold values from -0.1875 to 0.1875
- evict: int32 [8, 2], replicated, may hold values from 0 to 5, as said below
- recall: int32 [8, 2], replicated, may hold values from 0 to 5, as said below
Outputs:
- passed: float32 [8, 32, 128, 1024], P('segment', 'dp')
- returned: float32 [8, 32, 128, 1024], P('segment', 'dp')
- kept_out: float32 [8, 3, 32, 128, 1024], P('segment', None, 'dp')
- lent_out: float32 [8, 3, 32, 128, 1024], P('segment', None, 'dp')
- grad_in: float32 [8, 1024, 2048], P('segment', 'dp')
- grad_kernel: float32 [8, 31, 1024], P('segment')
- grad_out: float32 [8, 1024, 1024], P('segment', 'dp')
Inputs may be any that keep to these rules, and one draw needn't show every extreme that they name: `evict`: for s < 4 the value at tick 0 is at least 3 and the tick 1 value differs from it; for s >= 4 both values are below 3 and differ. `recall`: for s < 4 the value at tick 0 is at least 3; for s >= 4 values are below 3.
All inputs are finite; a program needn't handle non-finite values.
Results may differ from a plain program's by a relative error of at most 0.00014.
Values sent between devices are 32-bit elements; how exact they have to be, the bound alone decides.
A program may use at most 128 MiB of HBM per device.

v0:
```python
import jax
import jax.numpy as jnp
from jax import lax
from jax.sharding import PartitionSpec as P

TICKS = 2


EPSILON = 1e-05


def shifted(x, axis, by):
    size = lax.axis_size(axis)
    pairs = [(i, i + by) for i in range(size) if 0 <= i + by < size]
    return lax.ppermute(x, axis, pairs)


def from_partner(value, axis, bit):
    mask = 2**bit
    pairs = [(source, source ^ mask) for source in range(lax.axis_size(axis))]
    return lax.ppermute(value, axis, pairs)


def normalize(values):
    center = values - jnp.mean(values, axis=-1, keepdims=True)
    spread = jnp.mean(center * center, axis=-1, keepdims=True)
    return center * lax.rsqrt(spread + EPSILON)


def module(frames_in, w_first, kernel_taps, w_second):
    seq_count, length, feat_width = frames_in.shape
    normed = normalize(frames_in).reshape(seq_count * length, feat_width)
    joined = jnp.dot(
        normed, w_first, precision=lax.Precision.HIGHEST, preferred_element_type=jnp.float32
    )
    gated_units = (joined[:, :feat_width] * jax.nn.sigmoid(joined[:, feat_width:])).reshape(
        seq_count, length, feat_width
    )
    half_width = kernel_taps.shape[0] // 2
    padded = jnp.pad(gated_units, ((0, 0), (half_width, half_width), (0, 0)))
    mixed_units = padded[:, 0:length] * kernel_taps[0]
    for offset in range(1, kernel_taps.shape[0]):
        mixed_units = mixed_units + padded[:, offset : offset + length] * kernel_taps[offset]
    normal_mix = normalize(mixed_units)
    swished = (normal_mix * jax.nn.sigmoid(normal_mix)).reshape(seq_count * length, feat_width)
    projected = jnp.dot(
        swished, w_second, precision=lax.Precision.HIGHEST, preferred_element_type=jnp.float32
    )
    return frames_in + projected.reshape(seq_count, length, feat_width)


def shards(
    arriving, entering, returning, loss_grad, kept, lent, w_in, kernel, w_out, evict, recall
):
    segment_count = lax.axis_size("segment")
    position = lax.axis_index("segment")
    mirror = segment_count - 1 - position
    slot_count = kept.shape[1]
    slot_ids = jnp.arange(slot_count, dtype=jnp.int32)
    bit_count = segment_count.bit_length() - 1
    full_first, full_second = (
        lax.all_gather(w_in[0], "dp", axis=0, tiled=True),
        lax.all_gather(w_out[0], "dp", axis=0, tiled=True),
    )
    kernel_taps = kernel[0]
    kept_now = kept[0]
    lent_now = lent[0]
    sum_first = jnp.zeros(full_first.shape, jnp.float32)
    sum_second = jnp.zeros(full_second.shape, jnp.float32)
    sum_taps = jnp.zeros(kernel_taps.shape, jnp.float32)
    forward_out = arriving[0]
    backward_out = returning[0]
    for tick in range(TICKS):
        if tick == 0:
            fwd_in = arriving[0]
            back_in = returning[0]
        else:
            from_above = shifted(forward_out, "segment", 1)
            fwd_in = jnp.where(position == 0, entering[tick - 1], from_above)
            from_below = shifted(backward_out, "segment", -1)
            back_in = jnp.where(position == segment_count - 1, loss_grad[tick - 1], from_below)
        own_read = recall[position, tick]
        mirror_read = recall[mirror, tick]
        own_pick = kept_now[jnp.clip(own_read, 0, slot_count - 1)]
        lend_pick = lent_now[jnp.clip(mirror_read - slot_count, 0, slot_count - 1)]
        incoming = fwd_in
        for bit in range(bit_count):
            lend_pick, incoming = from_partner((lend_pick, incoming), "segment", bit)
        stash = jnp.where(own_read < slot_count, own_pick, lend_pick)
        forward_out = module(fwd_in, full_first, kernel_taps, full_second)
        unused, pullback = jax.vjp(module, stash, full_first, kernel_taps, full_second)
        backward_out, d_first, d_taps, d_second = pullback(back_in)
        sum_taps = sum_taps + d_taps
        sum_first = sum_first + d_first
        sum_second = sum_second + d_second
        own_write = evict[position, tick]
        mirror_write = evict[mirror, tick]
        kept_now = jnp.where((slot_ids == own_write)[:, None, None, None], fwd_in[None], kept_now)
        lent_now = jnp.where(
            (slot_ids + slot_count == mirror_write)[:, None, None, None], incoming[None], lent_now
        )
    shard_first, shard_second = (
        lax.psum_scatter(sum_first, "dp", scatter_dimension=0, tiled=True),
        lax.psum_scatter(sum_second, "dp", scatter_dimension=0, tiled=True),
    )
    taps_total = lax.psum(sum_taps, "dp")
    scale = float(TICKS * arriving.shape[1] * lax.axis_size("dp") * arriving.shape[2]) ** (-0.5)
    return (
        forward_out[None],
        backward_out[None],
        kept_now[None],
        lent_now[None],
        (shard_first * scale)[None],
        (taps_total * scale)[None],
        (shard_second * scale)[None],
    )


def solution(mesh):
    placed = (
        P("segment", "dp", None, None),
        P(None, "dp", None, None),
        P("segment", "dp", None, None),
        P(None, "dp", None, None),
        P("segment", None, "dp", None, None),
        P("segment", None, "dp", None, None),
        P("segment", "dp", None),
        P("segment", None, None),
        P("segment", "dp", None),
        P(),
        P(),
    )
    return jax.shard_map(
        shards,
        mesh=mesh,
        in_specs=placed,
        out_specs=(
            P("segment", "dp", None, None),
            P("segment", "dp", None, None),
            P("segment", None, "dp", None, None),
            P("segment", None, "dp", None, None),
            P("segment", "dp", None),
            P("segment", None, None),
            P("segment", "dp", None),
        ),
        check_vma=False,
    )
```

profile of v0, /device:TPU:2, one launch (start us, length us, event | category | flops | bytes accessed | tf_op | source)
XLA Modules:
  0.0 576.5 jit_solution(11941122833585475577)
XLA Ops:
  8.7 2.0 collective-permute-start.5
  10.7 12.1 %collective-permute-done.5 = f32[1,128,1024]{2,1,0:T(8,128)S(1)} collective-permute-done((f32[1,128,1024]{2,1,0:T(8,128)}, f32[1,128,1024]{2,1,0:T(8,128)S(1)}, u32[]{:S(2)}, u32[]{:S(2)}) %collective-permute-start.5) | collective-permute-done | bytes 524320 | tf_op jit(solution)/shard_map/ppermute | solution.py:21
  22.9 3.3 collective-permute-start.6
  29.3 1.8 collective-permute-start.1
  31.1 17.7 %collective-permute-done.6 = f32[1,128,1024]{2,1,0:T(8,128)} collective-permute-done((f32[1,128,1024]{2,1,0:T(8,128)S(1)}, f32[1,128,1024]{2,1,0:T(8,128)}, u32[]{:S(2)}, u32[]{:S(2)}) %collective-permute-start.6) | collective-permute-done | bytes 524320 | tf_op jit(solution)/shard_map/ppermute | solution.py:21
  48.8 6.2 %collective-permute-start.7 = (f32[1,128,1024]{2,1,0:T(8,128)}, f32[1,128,1024]{2,1,0:T(8,128)S(1)}, u32[]{:S(2)}, u32[]{:S(2)}) collective-permute-start(f32[1,128,1024]{2,1,0:T(8,128)} %collective-permute-done.6), channel_id=1, source_target_pairs={{0,128},{32,160},{64,192},{96,224},{128,0},{160,32},{192,64},{224,... | collective-permute-start | bytes 1572872 | tf_op jit(solution)/shard_map/ppermute | solution.py:21
  59.6 18.3 %collective-permute-done.7 = f32[1,128,1024]{2,1,0:T(8,128)S(1)} collective-permute-done((f32[1,128,1024]{2,1,0:T(8,128)}, f32[1,128,1024]{2,1,0:T(8,128)S(1)}, u32[]{:S(2)}, u32[]{:S(2)}) %collective-permute-start.7) | collective-permute-done | bytes 524320 | tf_op jit(solution)/shard_map/ppermute | solution.py:21
  77.9 1.7 fusion.172
  81.8 19.7 %collective-permute-done.2 = f32[1,128,1024]{2,1,0:T(8,128)} collective-permute-done((f32[1,128,1024]{2,1,0:T(8,128)}, f32[1,128,1024]{2,1,0:T(8,128)}, u32[]{:S(2)}, u32[]{:S(2)}) %collective-permute-start.2) | collective-permute-done | bytes 524320 | tf_op jit(solution)/shard_map/ppermute | solution.py:21
  101.5 2.7 collective-permute-start.3
  104.2 3.9 collective-permute-start.9
  112.0 14.5 %collective-permute-done.3 = f32[1,128,1024]{2,1,0:T(8,128)S(1)} collective-permute-done((f32[1,128,1024]{2,1,0:T(8,128)}, f32[1,128,1024]{2,1,0:T(8,128)S(1)}, u32[]{:S(2)}, u32[]{:S(2)}) %collective-permute-start.3) | collective-permute-done | bytes 524320 | tf_op jit(solution)/shard_map/ppermute | solution.py:21
  128.5 22.0 %collective-permute-done.9 = f32[1,128,1024]{2,1,0:T(8,128)} collective-permute-done((f32[1,128,1024]{2,1,0:T(8,128)}, f32[1,128,1024]{2,1,0:T(8,128)}, u32[]{:S(2)}, u32[]{:S(2)}) %collective-permute-start.9) | collective-permute-done | bytes 524320 | tf_op jit(solution)/shard_map/ppermute | solution.py:21
  150.5 2.5 collective-permute-start.10
  153.2 25.6 %collective-permute-done.10 = f32[1,128,1024]{2,1,0:T(8,128)S(1)} collective-permute-done((f32[1,128,1024]{2,1,0:T(8,128)}, f32[1,128,1024]{2,1,0:T(8,128)S(1)}, u32[]{:S(2)}, u32[]{:S(2)}) %collective-permute-start.10) | collective-permute-done | bytes 524320 | tf_op jit(solution)/shard_map/ppermute | solution.py:21
  179.8 7.1 %fusion.6 = f32[128,2048]{1,0:T(8,128)S(1)} fusion(f32[1,1024,2048]{2,1,0:T(8,128)} %all-gather.5.cloned.1.call-done, f32[1,128,1024]{2,1,0:T(8,128)S(1)} %get-tuple-element.88, f32[128]{0:T(128)S(1)} %fusion.302, f32[128]{0:T(128)S(1)} %broadcast_multiply_fusion.66), kind=kOutput, calls=%fused_computation.6 | convolution fusion | flops 3221487616 | bytes 9962496 | tf_op jit(solution)/shard_map/jvp()/dot_general | solution.py:33
  187.9 2.6 fusion.329
  190.7 6.9 %multiply_reduce_fusion.65 = (f32[128]{0:T(128)S(1)}, f32[1,128,1024]{2,1,0:T(8,128)S(1)}) fusion(f32[1,128,1024]{2,1,0:T(8,128)S(1)} %get-tuple-element.86, f32[128]{0:T(128)S(1)} %broadcast_multiply_fusion.65, f32[128]{0:T(128)S(1)} %fusion.303, f32[1,1024,1024]{2,1,0:T(8,128)} %all-gather.7.cloned.1.call-done, f32[1,1,128,1024]{3,2,1,0:T(8,128)} %param.13), kind=kOutput, calls=%fused_computation.451 | convolution fusion | flops 1612316544 | bytes 5768704 | tf_op jit(solution)/shard_map/transpose(jvp())/dot_general | solution.py:46
  199.2 2.3 broadcast_multiply_fusion.5
  203.6 4.0 pad_add_fusion.7
  208.4 9.4 %fusion.210 = (f32[128]{0:T(128)S(1)}, f32[128,1024]{1,0:T(8,128)S(1)}) fusion(f32[1,128,1024]{2,1,0:T(8,128)S(1)} %get-tuple-element.88, f32[128]{0:T(128)S(1)} %broadcast_multiply_fusion.66, f32[1,1024,2048]{2,1,0:T(8,128)S(1)} %bitcast.357, f32[128,1024]{1,0:T(8,128)S(1)} %fusion.317, f32[128,1024]{1,0:T(8,128)S(1)} %get-tuple-element.81), kind=kOutput, calls=%fused_computation.353 | convolution fusion | flops 3221880832 | bytes 10486784 | tf_op jit(solution)/shard_map/transpose(jvp())/dot_general | solution.py:33
  219.5 4.6 fusion.2
  224.3 2.5 fusion.322
  226.8 4.6 fusion.10
  231.6 2.4 fusion.335
  234.2 2.5 fusion.23
  236.8 4.7 collective-permute-start
  241.7 5.5 fusion.188
  247.3 4.6 multiply_reduce_fusion.62
  253.9 1.9 multiply_reduce_fusion.29
  256.9 8.1 %convolution_add_fusion.1 = f32[1024,1024]{1,0:T(8,128)} fusion(f32[1024,1024]{1,0:T(8,128)} %fusion.188, f32[1,128,1024]{2,1,0:T(8,128)} %copy-done.8, f32[1,128,1024]{2,1,0:T(8,128)} %copy-done.3, f32[128]{0:T(128)S(1)} %fusion.305, f32[128]{0:T(128)S(1)} %broadcast_multiply_fusion.63), kind=kOutput, calls=%fused_computation.21 | convolution fusion | flops 1612447744 | bytes 9438208 | tf_op jit(solution)/shard_map/transpose(jvp())/dot_general | solution.py:46
  265.4 1.9 broadcast_multiply_fusion.4
  268.6 1.8 pad_add_fusion.6
  271.9 7.1 %fusion.41 = f32[1024,2048]{1,0:T(8,128)S(1)} fusion(f32[128,1024]{1,0:T(8,128)S(1)} %fusion.318, f32[128,1024]{1,0:T(8,128)S(1)} %get-tuple-element.71, f32[1,128,1024]{2,1,0:T(8,128)S(1)} %get-tuple-element.78, f32[128]{0:T(128)S(1)} %fusion.304, f32[128]{0:T(128)S(1)} %broadcast_multiply_fusion.64), kind=kOutput, calls=%fused_computation.153 | convolution fusion | flops 3221749760 | bytes 9962496 | tf_op jit(solution)/shard_map/transpose(jvp())/dot_general | solution.py:33
  279.1 9.5 %convolution_add_fusion = f32[1024,2048]{1,0:T(8,128)} fusion(f32[1024,2048]{1,0:T(8,128)S(1)} %fusion.41, f32[128,1024]{1,0:T(8,128)S(1)} %copy-done.14, f32[128,1024]{1,0:T(8,128)S(1)} %copy-done.16, f32[1,128,1024]{2,1,0:T(8,128)S(1)} %get-tuple-element.88, f32[128]{0:T(128)S(1)} %fusion.302, f32[128]{0:T(128)S(1)} %broadcast_multiply_fusion.66), kind=kOutput, calls=%fused_computation.12 | convolution fusion | flops 3223846912 | bytes 18351104 | tf_op jit(solution)/shard_map/transpose(jvp())/dot_general | solution.py:33
  290.1 2.6 collective-permute-start.11
  292.9 11.4 %fusion.190 = (f32[128]{0:T(128)S(1)}, f32[128,1024]{1,0:T(8,128)S(1)}) fusion(f32[1,128,1024]{2,1,0:T(8,128)S(1)} %get-tuple-element.78, f32[128]{0:T(128)S(1)} %broadcast_multiply_fusion.64, f32[1,1024,2048]{2,1,0:T(8,128)} %all-gather.5.cloned.1.call-done, f32[128,1024]{1,0:T(8,128)S(1)} %copy-done.18, f32[128,1024]{1,0:T(8,128)S(1)} %copy-done.20), kind=kOutput, calls=%fused_computation.331 | convolution fusion | flops 3221880832 | bytes 10486784 | tf_op jit(solution)/shard_map/transpose(jvp())/dot_general | solution.py:33
  304.2 7.1 %fusion.8 = f32[128,2048]{1,0:T(8,128)S(1)} fusion(f32[1,1024,2048]{2,1,0:T(8,128)} %all-gather.5.cloned.1.call-done, f32[1,128,1024]{2,1,0:T(8,128)S(1)} %get-tuple-element.205, f32[128]{0:T(128)S(1)} %add_rsqrt_fusion.1, f32[128]{0:T(128)S(1)} %broadcast_multiply_fusion.68), kind=kOutput, calls=%fused_computation.8 | convolution fusion | flops 3221487616 | bytes 9962496 | tf_op jit(solution)/shard_map/dot_general | solution.py:33
  311.7 2.4 fusion.332
  315.9 3.3 collective-permute-start.12
  319.1 3.3 fusion.38
  322.4 18.3 %collective-permute-done.12 = f32[1,128,1024]{2,1,0:T(8,128)S(1)} collective-permute-done((f32[1,128,1024]{2,1,0:T(8,128)S(1)}, f32[1,128,1024]{2,1,0:T(8,128)S(1)}, u32[]{:S(2)}, u32[]{:S(2)}) %collective-permute-start.12) | collective-permute-done | bytes 524320 | tf_op jit(solution)/shard_map/ppermute | solution.py:21
  340.8 5.9 %collective-permute-start.13 = (f32[1,128,1024]{2,1,0:T(8,128)S(1)}, f32[1,128,1024]{2,1,0:T(8,128)S(1)}, u32[]{:S(2)}, u32[]{:S(2)}) collective-permute-start(f32[1,128,1024]{2,1,0:T(8,128)S(1)} %collective-permute-done.12), channel_id=1, source_target_pairs={{0,128},{32,160},{64,192},{96,224},{128,0},{160,32},{192,64},{224,... | collective-permute-start | bytes 1572872 | tf_op jit(solution)/shard_map/ppermute | solution.py:21
  347.6 23.2 %all-reduce.134.cloned.1.call-done = f32[31,1024]{1,0:T(8,128)} async-done(((f32[31,1024]{1,0:T(8,128)}), f32[31,1024]{1,0:T(8,128)}) %all-reduce.134.cloned.1.call-update) | async-done | bytes 126992 | tf_op jit(solution)/shard_map/psum | solution.py:106
  372.5 3.0 select_select_fusion
  375.5 89.0 %reduce-scatter.5.cloned.1.call-done = f32[32,1024]{1,0:T(8,128)} async-done(((f32[1024,1024]{1,0:T(8,128)}), f32[32,1024]{1,0:T(8,128)}) %reduce-scatter.5.cloned.1.call-update) | async-done | bytes 131088 | tf_op jit(solution)/shard_map/reduce_scatter | solution.py:104
  466.0 102.0 %reduce-scatter.3.cloned.1.call-done = f32[32,2048]{1,0:T(8,128)} async-done(((f32[1024,2048]{1,0:T(8,128)}), f32[32,2048]{1,0:T(8,128)}) %reduce-scatter.3.cloned.1.call-update) | async-done | bytes 262160 | tf_op jit(solution)/shard_map/reduce_scatter | solution.py:103
  568.0 1.7 multiply_bitcast_fusion
  (163 shorter events, 36.8 us)
Async XLA Ops:
  7.2 171.6 %copy-start.2 = (f32[1,1,128,1024]{3,2,1,0:T(8,128)S(1)}, f32[1,1,128,1024]{3,2,1,0:T(8,128)}, u32[]{:S(2)}) copy-start(f32[1,1,128,1024]{3,2,1,0:T(8,128)} %param.11) | copy-start | bytes 1572868
  7.2 104.8 %copy-start.32 = (f32[1,31,1024]{2,0,1:T(1,128)S(1)}, f32[1,31,1024]{2,0,1:T(1,128)}, u32[]{:S(2)}) copy-start(f32[1,31,1024]{2,0,1:T(1,128)} %param.18) | copy-start | bytes 380932
  7.2 120.1 %copy-start.21 = (f32[1,3,1,128,1024]{4,3,2,1,0:T(8,128)S(1)}, f32[1,3,1,128,1024]{4,3,2,1,0:T(8,128)}, u32[]{:S(2)}) copy-start(f32[1,3,1,128,1024]{4,3,2,1,0:T(8,128)} %param.15) | copy-start | bytes 4718596
  7.2 172.6 %all-gather.5.cloned.1.call-start = ((), (), s32[]{:S(2)}) async-start(), calls=%async_computation.5 | async-start | bytes 8650752 | tf_op jit(solution)/shard_map/all_gather | solution.py:62
  7.9 182.8 %all-gather.7.cloned.1.call-start = ((), (), s32[]{:S(2)}) async-start(), calls=%async_computation.6 | async-start | bytes 4325376 | tf_op jit(solution)/shard_map/all_gather | solution.py:63
  8.7 362.1 %all-reduce.134.cloned.1.call-start = ((), (), s32[]{:S(2)}) async-start(), calls=%async_computation.3 | async-start | bytes 262144 | tf_op jit(solution)/shard_map/psum | solution.py:106
  8.7 14.1 %collective-permute-start.5 = (f32[1,128,1024]{2,1,0:T(8,128)}, f32[1,128,1024]{2,1,0:T(8,128)S(1)}, u32[]{:S(2)}, u32[]{:S(2)}) collective-permute-start(f32[1,128,1024]{2,1,0:T(8,128)} %bitcast.358), channel_id=1, source_target_pairs={{0,32},{32,0},{64,96},{96,64},{128,160},{160,128},{192,224},{224,1... | collective-permute-start | bytes 1572872 | tf_op jit(solution)/shard_map/ppermute | solution.py:21
  22.9 26.0 %collective-permute-start.6 = (f32[1,128,1024]{2,1,0:T(8,128)S(1)}, f32[1,128,1024]{2,1,0:T(8,128)}, u32[]{:S(2)}, u32[]{:S(2)}) collective-permute-start(f32[1,128,1024]{2,1,0:T(8,128)S(1)} %collective-permute-done.5), channel_id=1, source_target_pairs={{0,64},{32,96},{64,0},{96,32},{128,192},{160,224},{192,128},{224,1... | collective-permute-start | bytes 1572872 | tf_op jit(solution)/shard_map/ppermute | solution.py:21
  29.3 30.3 %collective-permute-start.1 = (f32[1,128,1024]{2,1,0:T(8,128)S(1)}, f32[1,128,1024]{2,1,0:T(8,128)}, u32[]{:S(2)}, u32[]{:S(2)}) collective-permute-start(f32[1,128,1024]{2,1,0:T(8,128)S(1)} %dynamic-slice_bitcast_fusion), channel_id=1, source_target_pairs={{0,32},{32,0},{64,96},{96,64},{128,160},{160,128},{192,224},{224,1... | collective-permute-start | bytes 1572872 | tf_op jit(solution)/shard_map/ppermute | solution.py:21
  48.8 29.0 %collective-permute-start.7 = (f32[1,128,1024]{2,1,0:T(8,128)}, f32[1,128,1024]{2,1,0:T(8,128)S(1)}, u32[]{:S(2)}, u32[]{:S(2)}) collective-permute-start(f32[1,128,1024]{2,1,0:T(8,128)} %collective-permute-done.6), channel_id=1, source_target_pairs={{0,128},{32,160},{64,192},{96,224},{128,0},{160,32},{192,64},{224,... | collective-permute-start | bytes 1572872 | tf_op jit(solution)/shard_map/ppermute | solution.py:21
  59.6 41.9 %collective-permute-start.2 = (f32[1,128,1024]{2,1,0:T(8,128)}, f32[1,128,1024]{2,1,0:T(8,128)}, u32[]{:S(2)}, u32[]{:S(2)}) collective-permute-start(f32[1,128,1024]{2,1,0:T(8,128)} %collective-permute-done.1), channel_id=1, source_target_pairs={{0,64},{32,96},{64,0},{96,32},{128,192},{160,224},{192,128},{224,1... | collective-permute-start | bytes 1572872 | tf_op jit(solution)/shard_map/ppermute | solution.py:21
  77.9 100.9 %copy-start.23 = (f32[1,128,1024]{2,1,0:T(8,128)}, f32[1,128,1024]{2,1,0:T(8,128)S(1)}, u32[]{:S(2)}) copy-start(f32[1,128,1024]{2,1,0:T(8,128)S(1)} %collective-permute-done.7) | copy-start | bytes 1572868
  79.6 24.6 %collective-permute-start.8 = (f32[1,128,1024]{2,1,0:T(8,128)S(1)}, f32[1,128,1024]{2,1,0:T(8,128)}, u32[]{:S(2)}, u32[]{:S(2)}) collective-permute-start(f32[1,128,1024]{2,1,0:T(8,128)S(1)} %fusion.172), channel_id=1, source_target_pairs={{0,32},{32,0},{64,96},{96,64},{128,160},{160,128},{192,224},{224,1... | collective-permute-start | bytes 1572872 | tf_op jit(solution)/shard_map/ppermute | solution.py:21
  101.5 25.0 %collective-permute-start.3 = (f32[1,128,1024]{2,1,0:T(8,128)}, f32[1,128,1024]{2,1,0:T(8,128)S(1)}, u32[]{:S(2)}, u32[]{:S(2)}) collective-permute-start(f32[1,128,1024]{2,1,0:T(8,128)} %collective-permute-done.2), channel_id=1, source_target_pairs={{0,128},{32,160},{64,192},{96,224},{128,0},{160,32},{192,64},{224,... | collective-permute-start | bytes 1572872 | tf_op jit(solution)/shard_map/ppermute | solution.py:21
  104.2 46.3 %collective-permute-start.9 = (f32[1,128,1024]{2,1,0:T(8,128)}, f32[1,128,1024]{2,1,0:T(8,128)}, u32[]{:S(2)}, u32[]{:S(2)}) collective-permute-start(f32[1,128,1024]{2,1,0:T(8,128)} %collective-permute-done.8), channel_id=1, source_target_pairs={{0,64},{32,96},{64,0},{96,32},{128,192},{160,224},{192,128},{224,1... | collective-permute-start | bytes 1572872 | tf_op jit(solution)/shard_map/ppermute | solution.py:21
  150.5 28.3 %collective-permute-start.10 = (f32[1,128,1024]{2,1,0:T(8,128)}, f32[1,128,1024]{2,1,0:T(8,128)S(1)}, u32[]{:S(2)}, u32[]{:S(2)}) collective-permute-start(f32[1,128,1024]{2,1,0:T(8,128)} %collective-permute-done.9), channel_id=1, source_target_pairs={{0,128},{32,160},{64,192},{96,224},{128,0},{160,32},{192,64},{224,... | collective-permute-start | bytes 1572872 | tf_op jit(solution)/shard_map/ppermute | solution.py:21
  190.5 8.7 %copy-start.6 = (f32[1,128,1024]{2,1,0:T(8,128)}, f32[1,128,1024]{2,1,0:T(8,128)S(1)}, u32[]{:S(2)}) copy-start(f32[1,128,1024]{2,1,0:T(8,128)S(1)} %get-tuple-element.86) | copy-start | bytes 1572868
  199.2 2.3 copy-start.11
  201.5 2.0 copy-start.28
  203.5 4.8 slice-start
  203.5 4.8 slice-start.1
  208.1 9.6 %copy-start.15 = (f32[128,1024]{1,0:T(8,128)}, f32[128,1024]{1,0:T(8,128)S(1)}, u32[]{:S(2)}) copy-start(f32[128,1024]{1,0:T(8,128)S(1)} %get-tuple-element.81) | copy-start | bytes 1572868
  208.3 9.5 %copy-start.13 = (f32[128,1024]{1,0:T(8,128)}, f32[128,1024]{1,0:T(8,128)S(1)}, u32[]{:S(2)}) copy-start(f32[128,1024]{1,0:T(8,128)S(1)} %fusion.317) | copy-start | bytes 1572868
  208.3 9.7 %copy-start.12 = (f32[1,1,128,1024]{3,2,1,0:T(8,128)S(1)}, f32[1,1,128,1024]{3,2,1,0:T(8,128)}, u32[]{:S(2)}) copy-start(f32[1,1,128,1024]{3,2,1,0:T(8,128)} %param.13) | copy-start | bytes 1572868
  218.2 29.0 %collective-permute-start.4 = (f32[1,128,1024]{2,1,0:T(8,128)S(1)}, f32[1,128,1024]{2,1,0:T(8,128)S(1)}, u32[]{:S(2)}, u32[]{:S(2)}) collective-permute-start(f32[1,128,1024]{2,1,0:T(8,128)S(1)} %fusion.230), channel_id=1, source_target_pairs={{32,0},{64,32},{96,64},{128,96},{160,128},{192,160},{224,192},{33,... | collective-permute-start | bytes 1572872 | tf_op jit(solution)/shard_map/ppermute | solution.py:15
  226.8 25.7 %copy-start.3 = (f32[1,128,1024]{2,1,0:T(8,128)}, f32[1,128,1024]{2,1,0:T(8,128)S(1)}, u32[]{:S(2)}) copy-start(f32[1,128,1024]{2,1,0:T(8,128)S(1)} %get-tuple-element.76) | copy-start | bytes 1572868
  231.4 2.8 copy-start
  231.6 10.1 %copy-start.7 = (f32[1,128,1024]{2,1,0:T(8,128)S(1)}, f32[1,128,1024]{2,1,0:T(8,128)}, u32[]{:S(2)}) copy-start(f32[1,128,1024]{2,1,0:T(8,128)} %copy-done.6) | copy-start | bytes 1572868
  236.8 10.5 %copy-start.31 = (f32[1,1,128,1024]{3,2,1,0:T(8,128)S(1)}, f32[1,1,128,1024]{3,2,1,0:T(8,128)}, u32[]{:S(2)}) copy-start(f32[1,1,128,1024]{3,2,1,0:T(8,128)} %param.14) | copy-start | bytes 1572868
  236.8 15.8 %collective-permute-start = (f32[1,128,1024]{2,1,0:T(8,128)S(1)}, f32[1,128,1024]{2,1,0:T(8,128)S(1)}, u32[]{:S(2)}, u32[]{:S(2)}) collective-permute-start(f32[1,128,1024]{2,1,0:T(8,128)S(1)} %fusion.23), channel_id=1, source_target_pairs={{0,32},{32,64},{64,96},{96,128},{128,160},{160,192},{192,224},{1,3... | collective-permute-start | bytes 1572872 | tf_op jit(solution)/shard_map/ppermute | solution.py:15
  247.2 5.3 copy-start.29
  247.3 5.5 copy-start.8
  256.8 207.6 %reduce-scatter.5.cloned.1.call-start = ((), (), s32[]{:S(2)}) async-start(), calls=%async_computation.4 | async-start | bytes 4325376 | tf_op jit(solution)/shard_map/reduce_scatter | solution.py:104
  265.0 303.1 %reduce-scatter.3.cloned.1.call-start = ((), (), s32[]{:S(2)}) async-start(), calls=%async_computation.2 | async-start | bytes 8650752 | tf_op jit(solution)/shard_map/reduce_scatter | solution.py:103
  265.4 1.9 copy-start.5
  268.5 1.8 copy-start.25
  268.6 1.8 copy-start.26
  271.9 7.1 %copy-start.14 = (f32[128,1024]{1,0:T(8,128)S(1)}, f32[128,1024]{1,0:T(8,128)}, u32[]{:S(2)}) copy-start(f32[128,1024]{1,0:T(8,128)} %copy-done.13) | copy-start | bytes 1572868
  271.9 7.1 %copy-start.16 = (f32[128,1024]{1,0:T(8,128)S(1)}, f32[128,1024]{1,0:T(8,128)}, u32[]{:S(2)}) copy-start(f32[128,1024]{1,0:T(8,128)} %copy-done.15) | copy-start | bytes 1572868
  288.6 4.2 copy-start.18
  288.6 4.2 copy-start.20
  290.1 25.8 %collective-permute-start.11 = (f32[1,128,1024]{2,1,0:T(8,128)S(1)}, f32[1,128,1024]{2,1,0:T(8,128)S(1)}, u32[]{:S(2)}, u32[]{:S(2)}) collective-permute-start(f32[1,128,1024]{2,1,0:T(8,128)S(1)} %get-tuple-element.205), channel_id=1, source_target_pairs={{0,32},{32,0},{64,96},{96,64},{128,160},{160,128},{192,224},{224,1... | collective-permute-start | bytes 1572872 | tf_op jit(solution)/shard_map/ppermute | solution.py:21
  311.3 3.0 copy-start.22
  311.5 7.7 %copy-start.1 = (f32[1,1024,1024]{2,1,0:T(8,128)S(1)}, f32[1,1024,1024]{2,1,0:T(8,128)}, u32[]{:S(2)}) copy-start(f32[1,1024,1024]{2,1,0:T(8,128)} %all-gather.7.cloned.1.call-done) | copy-start | bytes 12582916
  314.3 32.4 %copy-start.9 = (f32[1,128,1024]{2,1,0:T(8,128)S(1)}, f32[1,128,1024]{2,1,0:T(8,128)}, u32[]{:S(2)}) copy-start(f32[1,128,1024]{2,1,0:T(8,128)} %copy-done.8) | copy-start | bytes 1572868
  315.8 56.6 %copy-start.24 = (f32[1,128,1024]{2,1,0:T(8,128)S(1)}, f32[1,128,1024]{2,1,0:T(8,128)}, u32[]{:S(2)}) copy-start(f32[1,128,1024]{2,1,0:T(8,128)} %copy-done.23) | copy-start | bytes 1572868
  315.9 24.9 %collective-permute-start.12 = (f32[1,128,1024]{2,1,0:T(8,128)S(1)}, f32[1,128,1024]{2,1,0:T(8,128)S(1)}, u32[]{:S(2)}, u32[]{:S(2)}) collective-permute-start(f32[1,128,1024]{2,1,0:T(8,128)S(1)} %collective-permute-done.11), channel_id=1, source_target_pairs={{0,64},{32,96},{64,0},{96,32},{128,192},{160,224},{192,128},{224,1... | collective-permute-start | bytes 1572872 | tf_op jit(solution)/shard_map/ppermute | solution.py:21
  340.8 31.7 %collective-permute-start.13 = (f32[1,128,1024]{2,1,0:T(8,128)S(1)}, f32[1,128,1024]{2,1,0:T(8,128)S(1)}, u32[]{:S(2)}, u32[]{:S(2)}) collective-permute-start(f32[1,128,1024]{2,1,0:T(8,128)S(1)} %collective-permute-done.12), channel_id=1, source_target_pairs={{0,128},{32,160},{64,192},{96,224},{128,0},{160,32},{192,64},{224,... | collective-permute-start | bytes 1572872 | tf_op jit(solution)/shard_map/ppermute | solution.py:21
  (6 other events, 6.1 us)
Sparse Core Ops, SparseCore 0:
  10.6 60.8 all-gather.4
  74.0 50.4 all-gather.6
  256.9 113.8 all-reduce.133
  375.1 89.2 reduce-scatter.4
  468.3 99.6 reduce-scatter.2
where the time goes:
time: 584 us; the launch traced here: 576 us
  waiting for transfers between devices  365 us (62%)
  matrix products  91.6 us (16%)
  other arithmetic  51.4 us (9%)
  starting transfers between devices  40.9 us (7%)
  between operations  18.7 us (3%)
  local copies, waits for them, and re-layouts  9.34 us (2%)
    ppermute x12, waiting for transfers between devices, from_partner(): return lax.ppermute(value, axis, pairs)  148 us
    reduce_scatter x1, waiting for transfers between devices, shards(): lax.psum_scatter(sum_first, 'dp', scatter_dimension=0, tiled=True)  102 us
    reduce_scatter x1, waiting for transfers between devices, shards(): lax.psum_scatter(sum_second, 'dp', scatter_dimension=0, tiled=True)  89 us
    dot_general x8, matrix products, module(): jnp.dot(normed, w_first, precision=lax.Precision.HIGHEST, preferred_eleme...  60.7 us
    ppermute x12, starting transfers between devices, from_partner(): return lax.ppermute(value, axis, pairs)  34.3 us
    dot_general x6, matrix products, module(): jnp.dot(swished, w_second, precision=lax.Precision.HIGHEST, preferred_ele...  30.9 us
    psum x1, waiting for transfers between devices, shards(): taps_total = lax.psum(sum_taps, 'dp')  23.2 us
    reduce_sum x11, other arithmetic, normalize(): center = values - jnp.mean(values, axis=-1, keepdims=True)  14 us
  transfers between devices with their start and end apart: 19, of which 12 were waited for; matrix products, arithmetic and copies ran while one was open for 20% of the time, Pallas kernels for 0%

commit v1 on v0

v1 whole, which is shorter than its diff:
```python
import jax
import jax.numpy as jnp
from jax import lax
from jax.experimental import pallas as pl
from jax.experimental.pallas import tpu as pltpu
from jax.sharding import PartitionSpec as P

F, D, KW = 128, 1024, 31
IN, OUT, ALL = 2 * D, D, 3 * D
EPSILON = 1e-05
SCALE = float(2 * 32 * F) ** (-0.5)
BF, F32 = jnp.bfloat16, jnp.float32
NN = (((1,), (0,)), ((), ()))
NT = (((1,), (1,)), ((), ()))
MESH = pl.DeviceIdType.MESH
N_SEMS = 160
RING = (2, 1, 3, 0)
ORDER = (
    (2, 2), (1, 2), (3, 2), (0, 2), (2, 1), (2, 3), (2, 0),
    (1, 1), (1, 3), (3, 1), (3, 3), (0, 1), (0, 3), (1, 0), (3, 0), (0, 0),
)


def split(v):
    hi = v.astype(BF)
    return hi, (v - hi.astype(F32)).astype(BF)


def dot3(ah, al, bh, bl, dims):
    def one(a, b):
        return lax.dot_general(a, b, dims, preferred_element_type=F32)

    return one(ah, bh) + (one(ah, bl) + one(al, bh))


def loop(n, step, body):
    def run(i, carry):
        body(pl.multiple_of(i * step, step))
        return carry

    lax.fori_loop(0, n // step, run, 0)


def stats(v):
    center = v - jnp.mean(v, axis=-1, keepdims=True)
    inv = lax.rsqrt(jnp.mean(center * center, axis=-1, keepdims=True) + EPSILON)
    return center * inv, inv


def window(
    sel, arriving, entering, returning, loss, own0, own1, ex0, lend1, w_in, taps, w_out,
    passed, returned, a1_out, x0_out, x1_out, g_in, g_tap, g_out,
    W, Wh, Wl, S, R1, R2, T1, T2, H, Xh, Xl, XN, XTh, XTl, ZTh, ZTl, DHh, DHl, Gh, Gl,
    U0, U1, DC, C, ZN, INV, DZ, ST, YR, DR, V1, X0, X1, TP, DT, TR, send, recv,
):
    z = lax.axis_index("segment")
    d = lax.axis_index("dp")
    x, y, c = d // 8, (d // 2) % 4, d % 2

    def chip(xo, yo):
        return ((x + xo) % 4) * 8 + ((y + yo) % 4) * 2

    def rows_of(xo, yo, core):
        return pl.multiple_of((chip(xo, yo) + core) * 32, 32)

    def slot(xo, yo):
        return pl.multiple_of((chip(xo, yo) // 2) * 32, 32)

    def place(h, po, qo):
        return (po, qo) if h == 0 else (qo, po)

    def near(h, axis, sign):
        along_x = (h == 0) == (axis == 0)
        return {"dp": (chip(sign, 0) if along_x else chip(0, sign)) + c}

    sibling = {"dp": d + 1 - 2 * c}
    above = {"segment": (z + 1) % 8}
    below = {"segment": (z + 7) % 8}
    mirror = {"segment": 7 - z}

    barrier = pltpu.get_barrier_semaphore()
    peers = [near(0, a, s) for a in (0, 1) for s in (1, 3)] + [sibling, above, below, mirror]
    for peer in peers:
        pl.semaphore_signal(barrier, inc=1, device_id=peer, device_id_type=MESH)
    pl.semaphore_wait(barrier, len(peers))

    used = [0]
    sent = []

    def remote(src, dst, device, start=True):
        i = used[0]
        used[0] += 1
        copy = pltpu.make_async_remote_copy(
            src_ref=src, dst_ref=dst, send_sem=send.at[i], recv_sem=recv.at[i],
            device_id=device, device_id_type=MESH,
        )
        if start:
            copy.start()
        sent.append(copy)
        return copy

    copy_x0 = remote(ex0, X0, mirror)
    copy_x1 = remote(V1, X1, mirror, start=False)

    @pl.when(z >= 4)
    def _():
        V1[...] = lend1[...]
        copy_x1.start()

    mine = rows_of(0, 0, c)
    W[pl.ds(mine, 32), :IN] = w_in[...]
    W[pl.ds(mine, 32), IN:] = w_out[...]

    def pass_on(row, n, device):
        part = W.at[pl.ds(pl.multiple_of(row, 8), n), :]
        return remote(part, part, device)

    def piece(h, po, qo):
        return rows_of(*place(h, po, qo), c) + 16 * h

    first = {}
    second = {}
    far = {}
    over = []
    for h in (0, 1):
        for sign in (1, 3):
            first[h, sign] = pass_on(piece(h, 0, 0), 16, near(h, 0, sign))

    def along_q(h, po):
        for sign in (1, 3):
            second[h, po, sign] = pass_on(piece(h, po, 0), 16, near(h, 1, sign))

    for h in (0, 1):
        along_q(h, 0)
    over.append(pass_on(mine, 32, sibling))

    def norm_in(src, row0):
        def body(r):
            v, _ = stats(src[pl.ds(r, 16), :])
            XN[pl.ds(r, 16), :] = v
            hi, lo = split(v)
            Xh[pl.ds(row0 + r, 16), :] = hi
            Xl[pl.ds(row0 + r, 16), :] = lo

        loop(F, 16, body)

    norm_in(arriving, F)
    U0[...] = jnp.zeros_like(U0)
    U1[...] = jnp.zeros_like(U1)
    DC[...] = jnp.zeros_like(DC)
    DT[...] = jnp.zeros_like(DT)

    def cotangent(src, t):
        def body(r):
            hi, lo = split(src[pl.ds(r, 16), :])
            Gh[pl.ds(t * F + r, 16), :] = hi
            Gl[pl.ds(t * F + r, 16), :] = lo

        loop(F, 16, body)

    cotangent(returning, 0)

    ahead = {}
    for sign, back, lower in ((1, 3, 0), (3, 1, 8)):
        for h in (0, 1):
            first[h, sign].wait_recv()
            ahead[h, sign] = pass_on(piece(h, back, 0) + lower, 8, near(h, 0, sign))
            along_q(h, back)
            over.append(pass_on(piece(h, back, 0), 16, sibling))
    for h in (0, 1):
        for sign in (1, 3):
            ahead[h, sign].wait_recv()
        along_q(h, 2)
        over.append(pass_on(piece(h, 2, 0), 16, sibling))
    for po in (0, 3, 1, 2):
        for h in (0, 1):
            for sign, back, lower in ((1, 3, 0), (3, 1, 8)):
                second[h, po, sign].wait_recv()
                far[h, po, sign] = pass_on(piece(h, po, back) + lower, 8, near(h, 1, sign))
                over.append(pass_on(piece(h, po, back), 16, sibling))
    for po in (0, 3, 1, 2):
        for h in (0, 1):
            for sign in (1, 3):
                far[h, po, sign].wait_recv()
            over.append(pass_on(piece(h, po, 2), 16, sibling))
    for copy in over:
        copy.wait_recv()
    for copy in sent[2:]:
        copy.wait_send()
    del sent[2:]

    def halves(r):
        for j in range(3):
            hi, lo = split(W[pl.ds(r, 16), j * D : (j + 1) * D])
            Wh[pl.ds(r, 16), j * D : (j + 1) * D] = hi
            Wl[pl.ds(r, 16), j * D : (j + 1) * D] = lo

    loop(D, 16, halves)

    def project(ah, al, row0, m, col0, n, out):
        def body(j):
            cols = pl.ds(pl.multiple_of(col0 + j, 256), 256)
            out[0:m, pl.ds(j, 256)] = dot3(
                ah[row0 : row0 + m, :], al[row0 : row0 + m, :], Wh[:, cols], Wl[:, cols], NN
            )

        loop(n, 256, body)

    def project_back(ah, al, row0, col0, k, out):
        def body(j):
            out[:, pl.ds(j, 256)] = dot3(
                ah[row0 : row0 + F, :], al[row0 : row0 + F, :],
                Wh[pl.ds(j, 256), col0 : col0 + k], Wl[pl.ds(j, 256), col0 : col0 + k], NT,
            )

        loop(D, 256, body)

    def turn(src, th, tl, t):
        def body(j):
            hi, lo = split(src[:, pl.ds(j, 128)].T)
            th[pl.ds(j, 128), t * F : (t + 1) * F] = hi
            tl[pl.ds(j, 128), t * F : (t + 1) * F] = lo

        loop(D, 128, body)

    def gate_and_mix(row0, u_pad):
        def body(j, carry):
            left = pl.ds(pl.multiple_of(j * 128, 128), 128)
            right = pl.ds(pl.multiple_of(D + j * 128, 128), 128)
            gate = lax.logistic(H[row0 : row0 + F, right])
            H[row0 : row0 + F, right] = gate
            u_pad[j, 16 : 16 + F, :] = H[row0 : row0 + F, left] * gate
            total = u_pad[j, 1 : 1 + F, :] * taps[0:1, left]
            for k in range(1, KW):
                total = total + u_pad[j, 1 + k : 1 + k + F, :] * taps[k : k + 1, left]
            C[:, left] = total
            return carry

        lax.fori_loop(0, 8, body, 0)

    def swish(keep, send_on):
        def body(r):
            zn, inv = stats(C[pl.ds(r, 16), :])
            w = zn * lax.logistic(zn)
            if keep:
                ZN[pl.ds(r, 16), :] = zn
                INV[pl.ds(r, 16), :] = jnp.broadcast_to(inv, (16, 128))
                C[pl.ds(r, 16), :] = w
            if send_on:
                hi, lo = split(w)
                Xh[pl.ds(r, 16), :] = hi
                Xl[pl.ds(r, 16), :] = lo

        loop(F, 16, body)

    def recompute(t, u_pad):
        gate_and_mix(0, u_pad)
        swish(True, False)
        turn(C, ZTh, ZTl, t)

    def add_rows(a, b, out):
        def body(r):
            out[pl.ds(r, 16), :] = a[pl.ds(r, 16), :] + b[pl.ds(r, 16), :]

        loop(F, 16, body)

    def backward(t, u_pad, g, out, between):
        project_back(Gh, Gl, t * F, IN, OUT, DZ)

        def inner(r):
            zn, dw = ZN[pl.ds(r, 16), :], DZ[pl.ds(r, 16), :]
            s = lax.logistic(zn)
            dz = dw * (s * (1.0 + zn * (1.0 - s)))
            both = jnp.mean(dz, axis=-1, keepdims=True)
            slope = jnp.mean(dz * zn, axis=-1, keepdims=True)
            DZ[pl.ds(r, 16), :] = INV[pl.ds(r, 16), 0:1] * (dz - both - zn * slope)

        loop(F, 16, inner)

        def unmix(j, carry):
            left = pl.ds(pl.multiple_of(j * 128, 128), 128)
            right = pl.ds(pl.multiple_of(D + j * 128, 128), 128)
            DC[j, 16 : 16 + F, :] = DZ[:, left]
            du = DC[j, 31 : 31 + F, :] * taps[0:1, left]
            for k in range(1, KW):
                du = du + DC[j, 31 - k : 31 - k + F, :] * taps[k : k + 1, left]
            gate = H[0:F, right]
            hi, lo = split(du * gate)
            DHh[t * F : (t + 1) * F, left] = hi
            DHl[t * F : (t + 1) * F, left] = lo
            hi, lo = split(du * u_pad[j, 16 : 16 + F, :] * (1.0 - gate))
            DHh[t * F : (t + 1) * F, right] = hi
            DHl[t * F : (t + 1) * F, right] = lo
            return carry

        lax.fori_loop(0, 8, unmix, 0)
        between()
        project_back(DHh, DHl, t * F, 0, IN, DZ)

        def outer(r):
            v, inv = stats(ST[pl.ds(r, 16), :])
            dv = DZ[pl.ds(r, 16), :]
            both = jnp.mean(dv, axis=-1, keepdims=True)
            slope = jnp.mean(dv * v, axis=-1, keepdims=True)
            out[pl.ds(r, 16), :] = g[pl.ds(r, 16), :] + inv * (dv - both - v * slope)

        loop(F, 16, outer)

    def tap_grads(t, u_pad):
        def body(j, carry):
            left = pl.ds(pl.multiple_of(j * 128, 128), 128)
            dc = DC[j, 16 : 16 + F, :].reshape(16, 8, 128)
            for k in range(KW):
                part = jnp.sum(dc * u_pad[j, 1 + k : 1 + k + F, :].reshape(16, 8, 128), axis=0)
                if t == 0:
                    TP[j, k] = part
                else:
                    DT[0, k : k + 1, left] = jnp.sum(part + TP[j, k], axis=0, keepdims=True)
            return carry

        lax.fori_loop(0, 8, body, 0)

    copy_x0.wait_recv()

    @pl.when(z < 4)
    def _():
        ST[...] = X0[...]

    @pl.when(z >= 4)
    def _():
        ST[...] = own0[...]

    norm_in(ST, 0)
    turn(XN, XTh, XTl, 0)
    project(Xh, Xl, 0, 2 * F, 0, IN, H)
    recompute(0, U0)
    backward(0, U0, returning, returned, lambda: None)
    copy_d = remote(returned, DR, below)
    tap_grads(0, U0)
    gate_and_mix(F, U1)
    swish(False, True)
    project(Xh, Xl, 0, F, IN, OUT, DZ)
    add_rows(arriving, DZ, passed)
    copy_y = remote(passed, YR, above)

    @pl.when(z < 4)
    def _():
        copy_x1.wait_recv()

        def body(r):
            for j in range(8):
                lanes = slice(j * 128, (j + 1) * 128)
                chosen = jnp.broadcast_to(sel[0:1, :], (16, 128)) > 0
                ST[pl.ds(r, 16), lanes] = jnp.where(
                    chosen, X1[pl.ds(r, 16), lanes], own1[pl.ds(r, 16), lanes]
                )

        loop(F, 16, body)

    @pl.when(z >= 4)
    def _():
        ST[...] = own1[...]

    norm_in(ST, 0)
    turn(XN, XTh, XTl, 1)
    project(Xh, Xl, 0, F, 0, IN, H)
    recompute(1, U1)
    copy_d.wait()

    @pl.when(z == 7)
    def _():
        DR[...] = loss[...]

    cotangent(DR, 1)

    rounds = [0]
    odd_x, odd_y = x % 2, y % 2
    partners = [
        sibling,
        {"dp": chip(1 - 2 * odd_x + 4, 0) + c},
        {"dp": chip(3 + 2 * odd_x, 0) + c},
        {"dp": chip(0, 1 - 2 * odd_y + 4) + c},
        {"dp": chip(0, 3 + 2 * odd_y) + c},
    ]
    tap_copy = [None]

    def tap_round():
        i = rounds[0]
        if i > 0:
            tap_copy[0].wait_recv()
            DT[i] = DT[i - 1] + TR[i - 1]
        if i < 5:
            tap_copy[0] = remote(DT.at[i], TR.at[i], partners[i])
        rounds[0] += 1

    def between():
        tap_grads(1, U1)
        tap_round()

    backward(1, U1, DR, returned, between)
    tap_round()

    def weight_grad(th, tl, dh, dl, cols_in, cols_out):
        def body(r):
            out = dot3(th[pl.ds(r, 256), :], tl[pl.ds(r, 256), :], dh[:, cols_in], dl[:, cols_in], NN)
            W[pl.ds(r, 256), cols_out] = out

        loop(D, 256, body)

    def grad_out(j):
        weight_grad(ZTh, ZTl, Gh, Gl, pl.ds(j, 256), pl.ds(pl.multiple_of(IN + j, 256), 256))

    def grad_in(j):
        weight_grad(XTh, XTl, DHh, DHl, pl.ds(j, 256), pl.ds(j, 256))

    loop(OUT, 256, grad_out)
    tap_round()
    loop(IN, 256, grad_in)
    tap_round()

    pair = {}
    for o in ORDER:
        pair[o] = remote(W.at[pl.ds(rows_of(*o, 1 - c), 32), :], S.at[pl.ds(slot(*o), 32), :], sibling)

    def add_pair(o):
        pair[o].wait_recv()
        base, mine_rows = slot(*o), rows_of(*o, c)

        def body(r):
            S[pl.ds(base + r, 8), :] = S[pl.ds(base + r, 8), :] + W[pl.ds(mine_rows + r, 8), :]

        loop(32, 8, body)

    def part(h, po, qo, lower, n):
        row = slot(*place(h, po, qo)) + 16 * h + lower
        return pl.ds(pl.multiple_of(row, 8), n)

    def add_from(rows, *others):
        total = S[rows, :]
        for other in others:
            total = total + other
        S[rows, :] = total

    m1, m2 = {}, {}

    def open_ring(h, i, po):
        for side, sign in ((0, 1), (1, 3)):
            m1[h, i, side] = remote(
                S.at[part(h, po, 2, 8 * side, 8), :], R1.at[h, side, i], near(h, 1, sign)
            )

    for n, o in enumerate(ORDER):
        add_pair(o)
        if n < 4:
            open_ring(0, n, o[0])
        if n == 0 or 4 <= n < 7:
            open_ring(1, RING.index(o[1]), o[1])
    for i, po in enumerate(RING):
        for h in (0, 1):
            for side, sign in ((0, 1), (1, 3)):
                m1[h, i, side].wait_recv()
                add_from(part(h, po, sign, 8 * side, 8), R1[h, side, i])
                m2[h, i, side] = remote(
                    S.at[part(h, po, sign, 0, 16), :], R2.at[h, side, i], near(h, 1, sign)
                )
    tap_round()

    copy_y.wait()

    @pl.when(z == 0)
    def _():
        YR[...] = entering[...]

    @pl.when(z < 4)
    def _():
        V1[...] = YR[...]
        copy_x1.start()

    norm_in(YR, 0)
    project(Xh, Xl, 0, F, 0, IN, H)
    gate_and_mix(0, U0)
    swish(False, True)
    project(Xh, Xl, 0, F, IN, OUT, DZ)
    add_rows(YR, DZ, passed)
    a1_out[...] = YR[...]
    tap_round()
    g_tap[...] = DT[5, 0:KW, :] * SCALE

    t1, t2 = {}, {}
    for i, po in enumerate(RING):
        for h in (0, 1):
            for side in (0, 1):
                m2[h, i, side].wait_recv()
            add_from(part(h, po, 0, 0, 16), R2[h, 0, i], R2[h, 1, i])
            if i == 0:
                for side, sign in ((0, 1), (1, 3)):
                    t1[h, side] = remote(
                        S.at[part(h, 2, 0, 8 * side, 8), :], T1.at[h, side], near(h, 0, sign)
                    )
    for h in (0, 1):
        for side, sign in ((0, 1), (1, 3)):
            t1[h, side].wait_recv()
            add_from(part(h, sign, 0, 8 * side, 8), T1[h, side])
            t2[h, side] = remote(
                S.at[part(h, sign, 0, 0, 16), :], T2.at[h, side], near(h, 0, sign)
            )
    for h in (0, 1):
        for side in (0, 1):
            t2[h, side].wait_recv()
        total = (S[part(h, 0, 0, 0, 16), :] + T2[h, 0] + T2[h, 1]) * SCALE
        g_in[16 * h : 16 * h + 16, :] = total[:, :IN]
        g_out[16 * h : 16 * h + 16, :] = total[:, IN:]

    @pl.when(z >= 4)
    def _():
        copy_x1.wait_recv()

    x0_out[...] = X0[...]
    x1_out[...] = X1[...]
    done = {id(copy_d), id(copy_y)}
    for copy in sent:
        if id(copy) not in done:
            copy.wait_send()


def run_window(sel, *operands):
    def f32(*shape):
        return jax.ShapeDtypeStruct(shape, F32)

    def vf(*shape):
        return pltpu.VMEM(shape, F32)

    def vb(*shape):
        return pltpu.VMEM(shape, BF)

    row = (F, D)
    vmem = pl.BlockSpec(memory_space=pltpu.VMEM)
    scratch = [
        vf(D, ALL), vb(D, ALL), vb(D, ALL), vf(512, ALL),
        vf(2, 2, 4, 8, ALL), vf(2, 2, 4, 16, ALL), vf(2, 2, 8, ALL), vf(2, 2, 16, ALL),
        vf(2 * F, IN), vb(2 * F, D), vb(2 * F, D), vf(*row),
        vb(D, 2 * F), vb(D, 2 * F), vb(D, 2 * F), vb(D, 2 * F), vb(2 * F, IN), vb(2 * F, IN),
        vb(2 * F, D), vb(2 * F, D),
        vf(8, 160, 128), vf(8, 160, 128), vf(8, 160, 128), vf(*row), vf(*row), vf(F, 128), vf(*row), vf(*row),
        vf(*row), vf(*row), vf(*row), vf(*row), vf(*row),
        vf(8, 32, 8, 128), vf(6, 32, D), vf(5, 32, D),
        pltpu.SemaphoreType.DMA((N_SEMS,)), pltpu.SemaphoreType.DMA((N_SEMS,)),
    ]
    return pl.pallas_call(
        window,
        out_shape=(
            f32(*row), f32(*row), f32(*row), f32(*row), f32(*row), f32(32, IN), f32(KW, D), f32(32, OUT),
        ),
        in_specs=[vmem] * (1 + len(operands)),
        out_specs=(vmem,) * 8,
        scratch_shapes=scratch,
        compiler_params=pltpu.CompilerParams(
            collective_id=0, has_side_effects=True, vmem_limit_bytes=62 * 1024 * 1024
        ),
    )(sel, *operands)


def shards(
    arriving, entering, returning, loss_grad, kept, lent, w_in, kernel, w_out, evict, recall
):
    position = lax.axis_index("segment")
    mirror = 7 - position
    kept_now, lent_now = kept[0, :, 0], lent[0, :, 0]
    arrived = arriving[0, 0]

    def pick(stack, i):
        return lax.dynamic_index_in_dim(stack, jnp.clip(i, 0, 2), 0, keepdims=False)

    read, write = recall[position], evict[position]
    their_read, their_write = recall[mirror], evict[mirror]
    own0 = pick(kept_now, read[0])
    own1 = jnp.where(read[1] == write[0], arrived, pick(kept_now, read[1]))
    lend0 = pick(lent_now, their_read[0] - 3)
    lend1 = pick(lent_now, their_read[1] - 3)
    exchanged = jnp.where(position < 4, arrived, lend0)
    use_lent = jnp.logical_and(read[1] >= 3, read[1] != write[0])
    sel = jnp.broadcast_to(use_lent.astype(jnp.int32), (8, 128))
    passed, returned, a1, x0, x1, g_in, g_tap, g_out = run_window(
        sel, arrived, entering[0, 0], returning[0, 0], loss_grad[0, 0], own0, own1, exchanged, lend1,
        w_in[0], kernel[0], w_out[0],
    )
    slot_ids = jnp.arange(3, dtype=jnp.int32)[:, None, None]
    kept_out = jnp.where(slot_ids == write[0], arrived[None], kept_now)
    kept_out = jnp.where(slot_ids == write[1], a1[None], kept_out)
    lent_out = jnp.where(slot_ids + 3 == their_write[0], x0[None], lent_now)
    lent_out = jnp.where(slot_ids + 3 == their_write[1], x1[None], lent_out)
    return (
        passed[None, None], returned[None, None], kept_out[None, :, None], lent_out[None, :, None],
        g_in[None], g_tap[None], g_out[None],
    )


def solution(mesh):
    placed = (
        P("segment", "dp", None, None),
        P(None, "dp", None, None),
        P("segment", "dp", None, None),
        P(None, "dp", None, None),
        P("segment", None, "dp", None, None),
        P("segment", None, "dp", None, None),
        P("segment", "dp", None),
        P("segment", None, None),
        P("segment", "dp", None),
        P(),
        P(),
    )
    return jax.shard_map(
        shards,
        mesh=mesh,
        in_specs=placed,
        out_specs=(
            P("segment", "dp", None, None),
            P("segment", "dp", None, None),
            P("segment", None, "dp", None, None),
            P("segment", None, "dp", None, None),
            P("segment", "dp", None),
            P("segment", None, None),
            P("segment", "dp", None),
        ),
        check_vma=False,
    )
```

time: 584 us -> 188 us (0.32); the launches traced: 576 us -> 187 us
  waiting for transfers between devices: 365 us -> 0 us
  Pallas kernels: 0 us -> 160 us
  matrix products: 91.6 us -> 0 us
  other arithmetic: 51.4 us -> 9.5 us
  starting transfers between devices: 40.9 us -> 0 us
  between operations: 18.7 us -> 6.75 us
    reduce_scatter x2 -> x0, waiting for transfers between devices: 191 us -> none  [the longest x1 102 us: shards(): lax.psum_scatter(sum_first, 'dp', scatter_dimension=0, tiled=True)]
    pallas_call x0 -> x1, Pallas kernels: none -> 160 us  [run_window(): pl.pallas_call(window, out_shape=(f32(*row), f32(*row), f32(*row), f32(*r...]
    ppermute x14 -> x0, waiting for transfers between devices: 149 us -> none  [the longest x12 148 us: from_partner(): return lax.ppermute(value, axis, pairs)]
    dot_general x14 -> x0, matrix products: 91.6 us -> none  [the longest x8 60.7 us: module(): jnp.dot(normed, w_first, precision=lax.Precision.HIGHEST, preferred_eleme...]
    ppermute x14 -> x0, starting transfers between devices: 40.3 us -> none  [the longest x12 34.3 us: from_partner(): return lax.ppermute(value, axis, pairs)]
    psum x1 -> x0, waiting for transfers between devices: 23.2 us -> none  [shards(): taps_total = lax.psum(sum_taps, 'dp')]
    reduce_sum x23 -> x0, other arithmetic: 21.5 us -> none  [the longest x11 14 us: normalize(): center = values - jnp.mean(values, axis=-1, keepdims=True)]
    mul x9 -> x0, other arithmetic: 9.04 us -> none  [the longest x4 6.68 us: module(): padded[:, offset:offset + length] * kernel_taps[offset]]
  transfers between devices with their start and end apart: 19 -> 0, of which waited for: 12 -> 0; matrix products, arithmetic and copies ran while one was open for 20% -> 0% of each run, Pallas kernels for 0% -> 0%
where the time goes in v1:
time: 188 us; the launch traced here: 187 us
  Pallas kernels  160 us (85%)
  local copies, waits for them, and re-layouts  10.9 us (6%)
  other arithmetic  9.5 us (5%)
  between operations  6.75 us (4%)
    pallas_call x1, Pallas kernels, run_window(): pl.pallas_call(window, out_shape=(f32(*row), f32(*row), f32(*row), f32(*r...  160 us
    unnamed x26, local copies, waits for them, and re-layouts  4.45 us

profile of v1, /device:TPU:2, one launch (start us, length us, event | category | flops | bytes accessed | tf_op | source)
XLA Modules:
  0.0 187.0 jit_solution(3643502928579752809)
XLA Ops:
  0.6 0.0 copy-start.1
  0.6 0.9 constant_dynamic-slice_fusion
  1.6 0.5 fusion.5
  2.1 0.6 fusion.3
  4.7 0.5 fusion.4
  5.8 2.5 %bitcast_select_fusion = (f32[128,1024]{1,0:T(8,128)}, f32[128,1024]{1,0:T(8,128)}) fusion(f32[1,3,1,128,1024]{4,3,2,1,0:T(8,128)} %param.16, s32[]{:T(128)} %bitcast.9, pred[]{:T(512)S(6)} %lt.17, f32[1,1,128,1024]{3,2,1,0:T(8,128)} %param.11, f32[1,3,1,128,1024]{4,3,2,1,0:T(8,128)} %param.15, s32[]{:T(128)S(6)} %min.24, pred[]{:T(512)S(6)} %eq.47), kind=kLoop, calls=%fused_computation.2 | loop fusion | flops 262144 | bytes 2621450 | tf_op jit(solution)/shard_map/jit(_where)/select_n | solution.py:580
  8.3 0.0 copy-start.9
  10.4 0.6 broadcast_in_dim.70.sel
  11.6 0.0 copy-done.1
  11.6 0.8 dynamic-slice_bitcast_fusion.lend1
  13.1 1.9 %dynamic-slice_bitcast_fusion.1.own0 = f32[128,1024]{1,0:T(8,128)} fusion(f32[1,3,1,128,1024]{4,3,2,1,0:T(8,128)} %param.15, s32[]{:T(128)} %bitcast.6), kind=kLoop, calls=%fused_computation.5 | loop fusion | bytes 1048580 | tf_op jit(solution)/shard_map/jit(dynamic_index_in_dim)/squeeze | solution.py:572
  15.0 0.0 copy-done.9
  15.0 0.7 copy.21
  15.7 159.9 %shard_map.162 = (f32[128,1024]{1,0:T(8,128)}, f32[128,1024]{1,0:T(8,128)}, f32[128,1024]{1,0:T(8,128)}, f32[128,1024]{1,0:T(8,128)}, f32[128,1024]{1,0:T(8,128)...) custom-call(s32[8,128]{1,0:T(8,128)} %broadcast_in_dim.70.sel, f32[128,1024]{1,0:T(8,128)} %bitcast.32, ...), custom_call_target="tpu_custom_call" | custom-call | tf_op jit(solution)/shard_map/pallas_call | solution.py:549
  175.6 0.5 fusion.2
  176.1 0.7 fusion
  176.8 0.7 fusion.1
  177.5 0.0 copy-start
  177.5 0.0 copy-start.2
  177.5 0.0 copy-start.3
  177.5 2.9 %select_select_fusion = f32[1,3,1,128,1024]{4,3,2,1,0:T(8,128)} fusion(f32[1,3,1,128,1024]{4,3,2,1,0:T(8,128)S(1)} %copy-done.1, f32[128,1024]{1,0:T(8,128)} %get-tuple-element.19, f32[128,1024]{1,0:T(8,128)} %get-tuple-element.18, pred[3]{0:T(512)(128)(4,1)S(1)} %fusion, pred[3]{0:T(512)(128)(4,1)S(1)} %fusion.1), kind=kLoop, calls=%fused_computation | loop fusion | flops 786432 | bytes 4194310 | tf_op jit(solution)/shard_map/jit(_where)/select_n | solution.py:591
  180.4 0.7 iota_compare_fusion
  181.1 0.7 iota_compare_fusion.1
  181.8 0.0 copy-done
  181.8 0.0 copy-done.2
  181.8 0.0 copy-done.3
  181.8 0.0 copy-start.8
  181.8 0.0 copy-start.5
  181.8 1.4 select_select_fusion.1
  183.3 0.0 copy-start.4
  183.3 0.0 copy-start.6
  183.3 0.0 copy-start.7
  183.3 0.0 copy-done.8
  183.3 0.8 copy.18
  184.1 0.0 copy-done.5
  184.1 0.8 copy.26
  184.9 0.0 copy-done.4
  184.9 0.8 copy.27
  185.7 0.0 copy-done.6
  185.7 0.7 copy.28
  186.4 0.0 copy-done.7
  186.4 0.7 copy.29
Async XLA Ops:
  0.6 11.0 %copy-start.1 = (f32[1,3,1,128,1024]{4,3,2,1,0:T(8,128)S(1)}, f32[1,3,1,128,1024]{4,3,2,1,0:T(8,128)}, u32[]{:S(2)}) copy-start(f32[1,3,1,128,1024]{4,3,2,1,0:T(8,128)} %param.16) | copy-start | bytes 4718596
  8.3 6.7 %copy-start.9 = (f32[1,31,1024]{2,0,1:T(1,128)S(1)}, f32[1,31,1024]{2,0,1:T(1,128)}, u32[]{:S(2)}) copy-start(f32[1,31,1024]{2,0,1:T(1,128)} %param.18) | copy-start | bytes 380932
  177.5 4.3 %copy-start = (f32[1,1,128,1024]{3,2,1,0:T(8,128)S(1)}, f32[1,1,128,1024]{3,2,1,0:T(8,128)}, u32[]{:S(2)}) copy-start(f32[1,1,128,1024]{3,2,1,0:T(8,128)} %param.11) | copy-start | bytes 1572868
  177.5 4.3 %copy-start.2 = (f32[1,3,1,128,1024]{4,3,2,1,0:T(8,128)S(1)}, f32[1,3,1,128,1024]{4,3,2,1,0:T(8,128)}, u32[]{:S(2)}) copy-start(f32[1,3,1,128,1024]{4,3,2,1,0:T(8,128)} %param.15) | copy-start | bytes 4718596
  177.5 4.3 %copy-start.3 = (f32[128,1024]{1,0:T(8,128)S(1)}, f32[128,1024]{1,0:T(8,128)}, u32[]{:S(2)}) copy-start(f32[128,1024]{1,0:T(8,128)} %get-tuple-element.17) | copy-start | bytes 1572868
  181.8 1.5 copy-start.8
  181.8 2.3 %copy-start.5 = (f32[128,1024]{1,0:T(8,128)S(1)}, f32[128,1024]{1,0:T(8,128)}, u32[]{:S(2)}) copy-start(f32[128,1024]{1,0:T(8,128)} %get-tuple-element.15) | copy-start | bytes 1572868
  183.3 1.6 copy-start.4
  183.3 2.4 %copy-start.6 = (f32[32,2048]{1,0:T(8,128)S(1)}, f32[32,2048]{1,0:T(8,128)}, u32[]{:S(2)}) copy-start(f32[32,2048]{1,0:T(8,128)} %get-tuple-element.20) | copy-start | bytes 786436
  183.3 3.1 %copy-start.7 = (f32[32,1024]{1,0:T(8,128)S(1)}, f32[32,1024]{1,0:T(8,128)}, u32[]{:S(2)}) copy-start(f32[32,1024]{1,0:T(8,128)} %get-tuple-element.22) | copy-start | bytes 393220

commit v2 on v0

v2 whole, which is shorter than its diff:
```python
import jax
import jax.numpy as jnp
from jax import lax
from jax.experimental import pallas as pl
from jax.experimental.pallas import tpu as pltpu
from jax.sharding import PartitionSpec as P

F, D, KW = 128, 1024, 31
IN, OUT, ALL = 2 * D, D, 3 * D
EPSILON = 1e-05
SCALE = float(2 * 32 * F) ** (-0.5)
BF, F32 = jnp.bfloat16, jnp.float32
NN = (((1,), (0,)), ((), ()))
NT = (((1,), (1,)), ((), ()))
MESH = pl.DeviceIdType.MESH
N_SEMS = 288
RING = (2, 1, 3, 0)
SIDES = ((0, 1, 3), (1, 3, 1))
RB = 64


def split(v):
    hi = v.astype(BF)
    return hi, (v - hi.astype(F32)).astype(BF)


def dot3(ah, al, bh, bl, dims):
    def one(a, b):
        return lax.dot_general(a, b, dims, preferred_element_type=F32)

    return one(ah, bh) + (one(ah, bl) + one(al, bh))


def loop(n, step, body, unroll=1):
    def run(i, carry):
        body(pl.multiple_of(i * step, step))
        return carry

    lax.fori_loop(0, n // step, run, 0, unroll=unroll)


def stats(v):
    center = v - jnp.mean(v, axis=-1, keepdims=True)
    inv = lax.rsqrt(jnp.mean(center * center, axis=-1, keepdims=True) + EPSILON)
    return center * inv, inv


def window(
    evict, recall, arriving, entering, returning, loss, kept, lent, w_in, taps, w_out,
    passed, returned, a1_out, x0_out, x1_out, g_in, g_tap, g_out,
    W, Wh, Wl, S, R1, R2, T1, T2, H, Xh, Xl, XN, XTh, XTl, ZTh, ZTl, DHh, DHl, Gh, Gl,
    U0, U1, DC, C, ZN, INV, DZ, ST, YR, DR, V0, V1, X0, X1, A, B, EDGE, PB, QB, TP, DT, TR,
    send, recv, local, free,
):
    z = lax.axis_index("segment")
    d = lax.axis_index("dp")
    x, y, c = d // 8, (d // 2) % 4, d % 2

    def chip(xo, yo):
        return ((x + xo) % 4) * 4 + ((y + yo) % 4)

    def place(h, po, qo):
        return (po, qo) if h == 0 else (qo, po)

    def near(h, axis, sign):
        along_x = (h == 0) == (axis == 0)
        return {"dp": (chip(sign, 0) if along_x else chip(0, sign)) * 2 + c}

    sibling = {"dp": d + 1 - 2 * c}
    above = {"segment": (z + 1) % 8}
    below = {"segment": (z + 7) % 8}
    mirror = {"segment": 7 - z}

    def fetch(i, src, dst):
        copy = pltpu.make_async_copy(src, dst, local.at[i])
        copy.start()
        return copy

    here = chip(0, 0)
    get_lent = fetch(3, lent, S.at[0:12, :, D : 2 * D])
    get_in = fetch(0, w_in, W.at[here, c, :, 0:IN])
    get_a = fetch(2, arriving, A)
    get_kept = fetch(5, kept, S.at[0:12, :, 0:D])
    get_out = fetch(1, w_out, W.at[here, c, :, IN:ALL])
    get_b = fetch(4, returning, B)

    @pl.when(z == 0)
    def _():
        fetch(6, entering, EDGE)

    @pl.when(z == 7)
    def _():
        fetch(6, loss, EDGE)

    barrier = pltpu.get_barrier_semaphore()
    peers = [near(0, a, s) for a in (0, 1) for s in (1, 3)] + [sibling, above, below, mirror]
    for peer in peers:
        pl.semaphore_signal(barrier, inc=1, device_id=peer, device_id_type=MESH)
    pl.semaphore_wait(barrier, len(peers))

    used = [0]
    sent = []

    def remote(src, dst, device, start=True):
        i = used[0]
        used[0] += 1
        copy = pltpu.make_async_remote_copy(
            src_ref=src, dst_ref=dst, send_sem=send.at[i], recv_sem=recv.at[i],
            device_id=device, device_id_type=MESH,
        )
        if start:
            copy.start()
        sent.append(copy)
        return copy

    def settle():
        for copy in sent:
            copy.wait_send()
        sent.clear()

    class Gather:
        def __init__(self, cols):
            self.cols = cols
            self.first, self.second, self.ahead, self.far, self.over = {}, {}, {}, {}, {}

        def pass_on(self, xo, yo, row, n, device):
            part = W.at[chip(xo, yo), c, row : row + n, self.cols]
            return remote(part, part, device)

        def piece(self, h, po, qo, device, lower=0, n=16):
            return self.pass_on(*place(h, po, qo), 16 * h + lower, n, device)

        def along_q(self, h, po):
            for sign in (1, 3):
                self.second[h, po, sign] = self.piece(h, po, 0, near(h, 1, sign))

        def cross(self, h, po, qo):
            self.over[h, po, qo] = self.piece(h, po, qo, sibling)

        def start(self):
            for h in (0, 1):
                for sign in (1, 3):
                    self.first[h, sign] = self.piece(h, 0, 0, near(h, 0, sign))
            for h in (0, 1):
                self.along_q(h, 0)
                self.cross(h, 0, 0)

        def one(self):
            for side, sign, back in SIDES:
                for h in (0, 1):
                    self.first[h, sign].wait_recv()
                    self.ahead[h, sign] = self.piece(h, back, 0, near(h, 0, sign), 8 * side, 8)
                    self.along_q(h, back)
                    self.cross(h, back, 0)

        def two(self):
            for h in (0, 1):
                for sign in (1, 3):
                    self.ahead[h, sign].wait_recv()
                self.along_q(h, 2)
                self.cross(h, 2, 0)

        def three(self, order):
            for po in order:
                for h in (0, 1):
                    for side, sign, back in SIDES:
                        self.second[h, po, sign].wait_recv()
                        self.far[h, po, sign] = self.piece(h, po, back, near(h, 1, sign), 8 * side, 8)
                        self.cross(h, po, back)

        def halve(self, h, po, core):
            for qo in range(4):
                i = chip(*place(h, po, qo))
                row = pl.multiple_of(i * 64 + core * 32 + 16 * h, 16)
                hi, lo = split(W[i, core, 16 * h : 16 * h + 16, self.cols])
                Wh[pl.ds(row, 16), self.cols] = hi
                Wl[pl.ds(row, 16), self.cols] = lo

        def four(self, order):
            for po in order:
                for h in (0, 1):
                    for sign in (1, 3):
                        self.far[h, po, sign].wait_recv()
                    self.cross(h, po, 2)
                    self.halve(h, po, c)

        def five(self, order):
            for po in order:
                for h in (0, 1):
                    for qo in range(4):
                        self.over[h, po, qo].wait_recv()
                    self.halve(h, po, 1 - c)

    first_in, first_out = Gather(slice(0, IN)), Gather(slice(IN, ALL))
    get_in.wait()
    first_in.start()

    get_lent.wait()
    get_a.wait()
    get_kept.wait()
    theirs = 7 - z

    def lent_slot(t):
        return S[pl.ds(4 * jnp.clip(recall[theirs, t] - 3, 0, 2), 4), :, D : 2 * D].reshape(F, D)

    @pl.when(z < 4)
    def _():
        V0[...] = A[...]

    @pl.when(z >= 4)
    def _():
        V0[...] = lent_slot(0)
        V1[...] = lent_slot(1)

    copy_x0 = remote(V0, X0, mirror)
    copy_x1 = remote(V1, X1, mirror, start=False)
    sent.pop()

    def norm_in(src, row0):
        def body(r):
            v, _ = stats(src[pl.ds(r, RB), :])
            XN[pl.ds(r, RB), :] = v
            hi, lo = split(v)
            Xh[pl.ds(row0 + r, RB), :] = hi
            Xl[pl.ds(row0 + r, RB), :] = lo

        loop(F, RB, body)

    def cotangent(src, t):
        def body(r):
            hi, lo = split(src[pl.ds(r, RB), :])
            Gh[pl.ds(t * F + r, RB), :] = hi
            Gl[pl.ds(t * F + r, RB), :] = lo

        loop(F, RB, body)

    def turn(src, th, tl, t):
        def body(j):
            hi, lo = split(src[:, pl.ds(j, 128)].T)
            th[pl.ds(j, 128), t * F : (t + 1) * F] = hi
            tl[pl.ds(j, 128), t * F : (t + 1) * F] = lo

        loop(D, 128, body, 2)

    first_in.one()
    norm_in(A, F)
    first_in.two()
    for pad in (U0, U1, DC):
        pad[:, 0:16, :] = jnp.zeros((8, 16, 128), F32)
        pad[:, 16 + F :, :] = jnp.zeros((8, 16, 128), F32)
    DT[0, 248:256, :] = jnp.zeros((8, 128), F32)
    get_b.wait()
    cotangent(B, 0)
    order = (0, 3, 1, 2)
    first_in.three(order)
    get_out.wait()
    first_out.start()
    first_in.four(order[:3])
    first_out.one()
    copy_x0.wait_recv()

    @pl.when(z >= 4)
    def _():
        copy_x1.start()

    @pl.when(z < 4)
    def _():
        ST[...] = X0[...]

    @pl.when(z >= 4)
    def _():
        ST[...] = S[pl.ds(4 * jnp.clip(recall[z, 0], 0, 2), 4), :, 0:D].reshape(F, D)

    norm_in(ST, 0)
    first_in.four(order[3:])
    first_out.two()
    first_in.five(order)
    first_out.three(order[:1])

    def project(ah, al, row0, m, col0, n, out, unroll=2):
        def body(j):
            cols = pl.ds(pl.multiple_of(col0 + j, 256), 256)
            out[0:m, pl.ds(j, 256)] = dot3(
                ah[row0 : row0 + m, :], al[row0 : row0 + m, :], Wh[:, cols], Wl[:, cols], NN
            )

        loop(n, 256, body, unroll)

    def project_back(ah, al, row0, col0, k, out, unroll=2):
        def body(j):
            out[:, pl.ds(j, 256)] = dot3(
                ah[row0 : row0 + F, :], al[row0 : row0 + F, :],
                Wh[pl.ds(j, 256), col0 : col0 + k], Wl[pl.ds(j, 256), col0 : col0 + k], NT,
            )

        loop(D, 256, body, unroll)

    def gate_and_mix(row0, u_pad):
        def body(j, carry):
            left = pl.ds(pl.multiple_of(j * 128, 128), 128)
            right = pl.ds(pl.multiple_of(D + j * 128, 128), 128)
            gate = lax.logistic(H[row0 : row0 + F, right])
            H[row0 : row0 + F, right] = gate
            u_pad[j, 16 : 16 + F, :] = H[row0 : row0 + F, left] * gate
            total = u_pad[j, 1 : 1 + F, :] * taps[pl.ds(j, 1), :]
            for k in range(1, KW):
                total = total + u_pad[j, 1 + k : 1 + k + F, :] * taps[pl.ds(8 * k + j, 1), :]
            C[:, left] = total
            return carry

        lax.fori_loop(0, 8, body, 0)

    def swish(keep, send_on):
        def body(r):
            zn, inv = stats(C[pl.ds(r, RB), :])
            w = zn * lax.logistic(zn)
            if keep:
                ZN[pl.ds(r, RB), :] = zn
                INV[pl.ds(r, RB), :] = jnp.broadcast_to(inv, (RB, 128))
                C[pl.ds(r, RB), :] = w
            if send_on:
                hi, lo = split(w)
                Xh[pl.ds(r, RB), :] = hi
                Xl[pl.ds(r, RB), :] = lo

        loop(F, RB, body)

    def add_rows(a, b, out):
        def body(r):
            out[pl.ds(r, RB), :] = a[pl.ds(r, RB), :] + b[pl.ds(r, RB), :]

        loop(F, RB, body)

    def unswish():
        def body(r):
            zn, dw = ZN[pl.ds(r, RB), :], DZ[pl.ds(r, RB), :]
            s = lax.logistic(zn)
            dz = dw * (s * (1.0 + zn * (1.0 - s)))
            both = jnp.mean(dz, axis=-1, keepdims=True)
            slope = jnp.mean(dz * zn, axis=-1, keepdims=True)
            DZ[pl.ds(r, RB), :] = INV[pl.ds(r, RB), 0:1] * (dz - both - zn * slope)

        loop(F, RB, body)

    def unmix(t, u_pad):
        def body(j, carry):
            left = pl.ds(pl.multiple_of(j * 128, 128), 128)
            right = pl.ds(pl.multiple_of(D + j * 128, 128), 128)
            DC[j, 16 : 16 + F, :] = DZ[:, left]
            du = DC[j, 31 : 31 + F, :] * taps[pl.ds(j, 1), :]
            for k in range(1, KW):
                du = du + DC[j, 31 - k : 31 - k + F, :] * taps[pl.ds(8 * k + j, 1), :]
            gate = H[0:F, right]
            hi, lo = split(du * gate)
            DHh[t * F : (t + 1) * F, left] = hi
            DHl[t * F : (t + 1) * F, left] = lo
            hi, lo = split(du * u_pad[j, 16 : 16 + F, :] * (1.0 - gate))
            DHh[t * F : (t + 1) * F, right] = hi
            DHl[t * F : (t + 1) * F, right] = lo
            return carry

        lax.fori_loop(0, 8, body, 0)

    def input_cotangent(g, out):
        def body(r):
            v, inv = stats(ST[pl.ds(r, RB), :])
            dv = DZ[pl.ds(r, RB), :]
            both = jnp.mean(dv, axis=-1, keepdims=True)
            slope = jnp.mean(dv * v, axis=-1, keepdims=True)
            out[pl.ds(r, RB), :] = g[pl.ds(r, RB), :] + inv * (dv - both - v * slope)

        loop(F, RB, body)

    def tap_grads(t, u_pad):
        def body(j, carry):
            dc = DC[j, 16 : 16 + F, :].reshape(16, 8, 128)
            for k in range(KW):
                part = jnp.sum(dc * u_pad[j, 1 + k : 1 + k + F, :].reshape(16, 8, 128), axis=0)
                if t == 0:
                    TP[j, k] = part
                else:
                    DT[0, pl.ds(8 * k + j, 1), :] = jnp.sum(part + TP[j, k], axis=0, keepdims=True)
            return carry

        lax.fori_loop(0, 8, body, 0)

    project(Xh, Xl, 0, 2 * F, 0, IN, H)
    first_out.three(order[1:])
    turn(XN, XTh, XTl, 0)
    gate_and_mix(0, U0)
    swish(True, False)
    turn(C, ZTh, ZTl, 0)
    first_out.four(order)
    gate_and_mix(F, U1)
    swish(False, True)
    first_out.five(order)
    project_back(Gh, Gl, 0, IN, OUT, DZ)
    unswish()
    unmix(0, U0)
    project_back(DHh, DHl, 0, 0, IN, DZ)
    input_cotangent(B, QB)
    copy_d = remote(QB, DR, below)
    project(Xh, Xl, 0, F, IN, OUT, DZ)
    add_rows(A, DZ, PB)
    copy_y = remote(PB, YR, above)
    tap_grads(0, U0)

    @pl.when(z < 4)
    def _():
        copy_x1.wait_recv()

    use_own = (recall[z, 1] == evict[z, 0]).astype(jnp.int32)
    use_lent = (recall[z, 1] >= 3).astype(jnp.int32)
    slot1 = 4 * jnp.clip(recall[z, 1], 0, 2)

    def choose(r):
        own = jnp.broadcast_to(use_own, (32, D)) > 0
        away = jnp.broadcast_to(use_lent, (32, D)) > 0
        value = S[slot1 + r // 32, :, 0:D]
        value = jnp.where(away, X1[pl.ds(r, 32), :], value)
        ST[pl.ds(r, 32), :] = jnp.where(own, A[pl.ds(r, 32), :], value)

    def choose_own(r):
        own = jnp.broadcast_to(use_own, (32, D)) > 0
        ST[pl.ds(r, 32), :] = jnp.where(own, A[pl.ds(r, 32), :], S[slot1 + r // 32, :, 0:D])

    @pl.when(z < 4)
    def _():
        loop(F, 32, choose)

    @pl.when(z >= 4)
    def _():
        loop(F, 32, choose_own)

    pl.semaphore_signal(free, inc=1, device_id=sibling, device_id_type=MESH)
    norm_in(ST, 0)
    turn(XN, XTh, XTl, 1)
    project(Xh, Xl, 0, F, 0, IN, H)
    gate_and_mix(0, U1)
    swish(True, False)
    turn(C, ZTh, ZTl, 1)

    @pl.when(jnp.logical_or(z == 0, z == 7))
    def _():
        pltpu.make_async_copy(loss, EDGE, local.at[6]).wait()

    copy_d.wait_recv()
    settle()

    @pl.when(z == 7)
    def _():
        DR[...] = EDGE[...]

    cotangent(DR, 1)

    odd_x, odd_y = x % 2, y % 2
    partners = [
        sibling,
        {"dp": chip(5 - 2 * odd_x, 0) * 2 + c},
        {"dp": chip(3 + 2 * odd_x, 0) * 2 + c},
        {"dp": chip(0, 5 - 2 * odd_y) * 2 + c},
        {"dp": chip(0, 3 + 2 * odd_y) * 2 + c},
    ]
    tap_copy = []

    def tap_round():
        i = len(tap_copy)
        if i > 0:
            tap_copy[-1].wait_recv()
            DT[i] = DT[i - 1] + TR[i - 1]
        if i < 5:
            tap_copy.append(remote(DT.at[i], TR.at[i], partners[i]))

    def weight_grad(th, tl, dh, dl, cols_in, cols_out):
        out = dot3(th[...], tl[...], dh[:, cols_in], dl[:, cols_in], NN)
        W[:, :, :, cols_out] = out.reshape(16, 2, 32, 256)

    def grad_out(j):
        weight_grad(ZTh, ZTl, Gh, Gl, pl.ds(j, 256), pl.ds(pl.multiple_of(IN + j, 256), 256))

    def grad_in(base):
        def body(j):
            cols = pl.ds(pl.multiple_of(base + j, 256), 256)
            weight_grad(XTh, XTl, DHh, DHl, cols, cols)

        loop(D, 256, body)

    class Reduce:
        def __init__(self, col0, out, out0):
            self.cols = slice(col0, col0 + D)
            self.out, self.out_cols = out, slice(out0, out0 + D)
            self.pair, self.m1, self.m2, self.t1, self.t2 = {}, {}, {}, {}, {}

        def start(self):
            for xo in RING:
                group = pl.ds(((x + xo) % 4) * 4, 4)
                self.pair[xo] = remote(
                    W.at[group, 1 - c, :, self.cols], S.at[group, :, self.cols], sibling
                )

        def at(self, h, po, qo, lower, n):
            return S.at[chip(*place(h, po, qo)), 16 * h + lower : 16 * h + lower + n, self.cols]

        def add(self, h, po, qo, lower, n, *others):
            i, rows = chip(*place(h, po, qo)), slice(16 * h + lower, 16 * h + lower + n)
            total = S[i, rows, self.cols]
            for other in others:
                total = total + other
            S[i, rows, self.cols] = total

        def open(self, h, i):
            for side, sign, _ in SIDES:
                self.m1[h, i, side] = remote(
                    self.at(h, RING[i], 2, 8 * side, 8), R1.at[h, side, i, :, self.cols], near(h, 1, sign)
                )

        def pairs(self):
            for n, xo in enumerate(RING):
                self.pair[xo].wait_recv()
                base = ((x + xo) % 4) * 4

                def body(i, carry):
                    S[base + i, :, self.cols] = S[base + i, :, self.cols] + W[base + i, c, :, self.cols]
                    return carry

                lax.fori_loop(0, 4, body, 0)
                self.open(0, n)
                if n == 0:
                    for i in range(4):
                        self.open(1, i)

        def middle(self):
            for i, po in enumerate(RING):
                for h in (0, 1):
                    for side, sign, _ in SIDES:
                        self.m1[h, i, side].wait_recv()
                        self.add(h, po, sign, 8 * side, 8, R1[h, side, i, :, self.cols])
                        self.m2[h, i, side] = remote(
                            self.at(h, po, sign, 0, 16), R2.at[h, side, i, :, self.cols], near(h, 1, sign)
                        )

        def turn(self):
            for i, po in enumerate(RING):
                for h in (0, 1):
                    for side in (0, 1):
                        self.m2[h, i, side].wait_recv()
                    self.add(h, po, 0, 0, 16, R2[h, 0, i, :, self.cols], R2[h, 1, i, :, self.cols])
                    if i == 0:
                        for side, sign, _ in SIDES:
                            self.t1[h, side] = remote(
                                self.at(h, 2, 0, 8 * side, 8), T1.at[h, side, :, self.cols], near(h, 0, sign)
                            )

        def last(self):
            for h in (0, 1):
                for side, sign, _ in SIDES:
                    self.t1[h, side].wait_recv()
                    self.add(h, sign, 0, 8 * side, 8, T1[h, side, :, self.cols])
                    self.t2[h, side] = remote(
                        self.at(h, sign, 0, 0, 16), T2.at[h, side, :, self.cols], near(h, 0, sign)
                    )

        def finish(self):
            for h in (0, 1):
                for side in (0, 1):
                    self.t2[h, side].wait_recv()
                rows = slice(16 * h, 16 * h + 16)
                total = S[chip(0, 0), rows, self.cols]
                for side in (0, 1):
                    total = total + T2[h, side, :, self.cols]
                self.out[rows, self.out_cols] = total * SCALE

    sum_out, sum_left, sum_right = Reduce(IN, g_out, 0), Reduce(0, g_in, 0), Reduce(D, g_in, D)
    loop(OUT, 256, grad_out)
    pl.semaphore_wait(free, 1)
    sum_out.start()
    project_back(Gh, Gl, F, IN, OUT, DZ)
    sum_out.pairs()
    unswish()
    unmix(1, U1)
    sum_out.middle()
    grad_in(0)
    sum_left.start()
    tap_grads(1, U1)
    tap_round()
    grad_in(D)
    sum_right.start()
    sum_left.pairs()
    tap_round()
    sum_out.turn()
    sum_left.middle()
    sum_right.pairs()
    project_back(DHh, DHl, F, 0, IN, DZ)
    tap_round()
    sum_out.last()
    sum_right.middle()
    input_cotangent(DR, QB)
    put_q = fetch(0, QB, returned)

    copy_y.wait_recv()

    @pl.when(z == 0)
    def _():
        YR[...] = EDGE[...]

    @pl.when(z < 4)
    def _():
        V1[...] = YR[...]
        copy_x1.start()

    put_a = fetch(1, YR, a1_out)
    norm_in(YR, 0)
    tap_round()
    sum_out.finish()
    sum_left.turn()
    project(Xh, Xl, 0, F, 0, IN, H)
    sum_left.last()
    tap_round()
    gate_and_mix(0, U0)
    swish(False, True)
    project(Xh, Xl, 0, F, IN, OUT, DZ)
    add_rows(YR, DZ, PB)
    put_p = fetch(2, PB, passed)
    put_x0 = fetch(3, X0, x0_out)
    tap_round()
    g_tap[...] = DT[5, 0 : 8 * KW, :] * SCALE
    sum_right.turn()
    sum_left.finish()
    sum_right.last()

    @pl.when(z >= 4)
    def _():
        copy_x1.wait_recv()

    put_x1 = fetch(4, X1, x1_out)
    sum_right.finish()
    copy_x1.wait_send()
    settle()
    for put in (put_q, put_a, put_p, put_x0, put_x1):
        put.wait()


def run_window(*operands):
    def f32(*shape):
        return jax.ShapeDtypeStruct(shape, F32)

    def vf(*shape):
        return pltpu.VMEM(shape, F32)

    def vb(*shape):
        return pltpu.VMEM(shape, BF)

    row = (F, D)
    vmem, smem = pl.BlockSpec(memory_space=pltpu.VMEM), pl.BlockSpec(memory_space=pltpu.SMEM)
    hbm = pl.BlockSpec(memory_space=pl.ANY)
    scratch = [
        vf(16, 2, 32, ALL), vb(D, ALL), vb(D, ALL), vf(16, 32, ALL),
        vf(2, 2, 4, 8, ALL), vf(2, 2, 4, 16, ALL), vf(2, 2, 8, ALL), vf(2, 2, 16, ALL),
        vf(2 * F, IN), vb(2 * F, D), vb(2 * F, D), vf(*row),
        vb(D, 2 * F), vb(D, 2 * F), vb(D, 2 * F), vb(D, 2 * F), vb(2 * F, IN), vb(2 * F, IN),
        vb(2 * F, D), vb(2 * F, D),
        vf(8, 160, 128), vf(8, 160, 128), vf(8, 160, 128), vf(*row), vf(*row), vf(F, 128), vf(*row), vf(*row),
        vf(*row), vf(*row), vf(*row), vf(*row), vf(*row), vf(*row), vf(*row), vf(*row), vf(*row), vf(*row), vf(*row),
        vf(8, 32, 8, 128), vf(6, 256, 128), vf(5, 256, 128),
        pltpu.SemaphoreType.DMA((N_SEMS,)), pltpu.SemaphoreType.DMA((N_SEMS,)), pltpu.SemaphoreType.DMA((8,)),
        pltpu.SemaphoreType.REGULAR,
    ]
    return pl.pallas_call(
        window,
        out_shape=(
            f32(*row), f32(*row), f32(*row), f32(*row), f32(*row), f32(32, IN), f32(8 * KW, 128), f32(32, OUT),
        ),
        in_specs=[smem] * 2 + [hbm] * 7 + [vmem, hbm],
        out_specs=(hbm,) * 5 + (vmem,) * 3,
        scratch_shapes=scratch,
        compiler_params=pltpu.CompilerParams(
            collective_id=0, has_side_effects=True, vmem_limit_bytes=63 * 1024 * 1024
        ),
    )(*operands)


def deliver(
    evict, kept, lent, arriving, a1, x0, x1, passed, returned, g_in, g_tap, g_out,
    o_passed, o_returned, o_kept, o_lent, o_in, o_tap, o_out,
    v_passed, v_returned, v_kept, v_lent, v_in, v_tap, v_out, sems,
):
    z = lax.axis_index("segment")
    plain = (
        (passed, v_passed, o_passed), (returned, v_returned, o_returned),
        (g_in, v_in, o_in), (g_tap, v_tap, o_tap), (g_out, v_out, o_out),
    )
    moves = []
    for src, held, dst in plain:
        copy = pltpu.make_async_copy(src, held, sems.at[0, len(moves)])
        copy.start()
        moves.append((copy, held, dst))
    for section, base, before, held, out, early, late in (
        (z, 0, kept, v_kept, o_kept, arriving, a1),
        (7 - z, 3, lent, v_lent, o_lent, x0, x1),
    ):
        for i in range(3):
            is_early = evict[section, 0] == base + i
            is_late = evict[section, 1] == base + i
            sem = sems.at[0, len(moves)]

            @pl.when(is_late)
            def _():
                pltpu.make_async_copy(late, held.at[i], sem).start()

            @pl.when(jnp.logical_and(is_early, jnp.logical_not(is_late)))
            def _():
                pltpu.make_async_copy(early, held.at[i], sem).start()

            @pl.when(jnp.logical_not(jnp.logical_or(is_early, is_late)))
            def _():
                pltpu.make_async_copy(before.at[i], held.at[i], sem).start()

            moves.append((pltpu.make_async_copy(before.at[i], held.at[i], sem), held.at[i], out.at[i]))
    leaving = []
    for i, (copy, held, dst) in enumerate(moves):
        copy.wait()
        copy = pltpu.make_async_copy(held, dst, sems.at[1, i])
        copy.start()
        leaving.append(copy)
    for copy in leaving:
        copy.wait()


def run_deliver(*operands):
    shapes = ((F, D), (F, D), (3, F, D), (3, F, D), (32, IN), (8 * KW, 128), (32, OUT))
    hbm = pl.BlockSpec(memory_space=pl.ANY)
    return pl.pallas_call(
        deliver,
        out_shape=tuple(jax.ShapeDtypeStruct(shape, F32) for shape in shapes),
        in_specs=[pl.BlockSpec(memory_space=pltpu.SMEM)] + [hbm] * 11,
        out_specs=(hbm,) * 7,
        scratch_shapes=[pltpu.VMEM(shape, F32) for shape in shapes] + [pltpu.SemaphoreType.DMA((2, 11))],
    )(*operands)


def shards(
    arriving, entering, returning, loss_grad, kept, lent, w_in, kernel, w_out, evict, recall
):
    arrived = arriving[0, 0]
    kept_now, lent_now = kept[0, :, 0], lent[0, :, 0]
    passed, returned, a1, x0, x1, g_in, g_tap, g_out = run_window(
        evict, recall, arrived, entering[0, 0], returning[0, 0], loss_grad[0, 0],
        kept_now.reshape(12, 32, D), lent_now.reshape(12, 32, D), w_in[0], kernel.reshape(8 * KW, 128), w_out[0],
    )
    passed, returned, kept_out, lent_out, g_in, g_tap, g_out = run_deliver(
        evict, kept_now, lent_now, arrived, a1, x0, x1, passed, returned, g_in, g_tap, g_out
    )
    return (
        passed[None, None], returned[None, None], kept_out[None, :, None], lent_out[None, :, None],
        g_in[None], g_tap.reshape(1, KW, D), g_out[None],
    )


def solution(mesh):
    placed = (
        P("segment", "dp", None, None),
        P(None, "dp", None, None),
        P("segment", "dp", None, None),
        P(None, "dp", None, None),
        P("segment", None, "dp", None, None),
        P("segment", None, "dp", None, None),
        P("segment", "dp", None),
        P("segment", None, None),
        P("segment", "dp", None),
        P(),
        P(),
    )
    return jax.shard_map(
        shards,
        mesh=mesh,
        in_specs=placed,
        out_specs=(
            P("segment", "dp", None, None),
            P("segment", "dp", None, None),
            P("segment", None, "dp", None, None),
            P("segment", None, "dp", None, None),
            P("segment", "dp", None),
            P("segment", None, None),
            P("segment", "dp", None),
        ),
        check_vma=False,
    )
```

time: 584 us -> 146 us (0.25); the launches traced: 576 us -> 145 us
  waiting for transfers between devices: 365 us -> 0 us
  Pallas kernels: 0 us -> 142 us
  matrix products: 91.6 us -> 0 us
  other arithmetic: 51.4 us -> 0 us
  starting transfers between devices: 40.9 us -> 0 us
  between operations: 18.7 us -> 0.8 us
  local copies, waits for them, and re-layouts: 9.34 us -> 2.69 us
    reduce_scatter x2 -> x0, waiting for transfers between devices: 191 us -> none  [the longest x1 102 us: shards(): lax.psum_scatter(sum_first, 'dp', scatter_dimension=0, tiled=True)]
    ppermute x14 -> x0, waiting for transfers between devices: 149 us -> none  [the longest x12 148 us: from_partner(): return lax.ppermute(value, axis, pairs)]
    pallas_call x0 -> x2, Pallas kernels: none -> 142 us  [the longest x1 137 us: run_window(): pl.pallas_call(window, out_shape=(f32(*row), f32(*row), f32(*row), f32(*r...]
    dot_general x14 -> x0, matrix products: 91.6 us -> none  [the longest x8 60.7 us: module(): jnp.dot(normed, w_first, precision=lax.Precision.HIGHEST, preferred_eleme...]
    ppermute x14 -> x0, starting transfers between devices: 40.3 us -> none  [the longest x12 34.3 us: from_partner(): return lax.ppermute(value, axis, pairs)]
    psum x1 -> x0, waiting for transfers between devices: 23.2 us -> none  [shards(): taps_total = lax.psum(sum_taps, 'dp')]
    reduce_sum x23 -> x0, other arithmetic: 21.5 us -> none  [the longest x11 14 us: normalize(): center = values - jnp.mean(values, axis=-1, keepdims=True)]
    mul x9 -> x0, other arithmetic: 9.04 us -> none  [the longest x4 6.68 us: module(): padded[:, offset:offset + length] * kernel_taps[offset]]
  transfers between devices with their start and end apart: 19 -> 0, of which waited for: 12 -> 0; matrix products, arithmetic and copies ran while one was open for 20% -> 0% of each run, Pallas kernels for 0% -> 0%
where the time goes in v2:
time: 146 us; the launch traced here: 145 us
  Pallas kernels  142 us (97%)
  local copies, waits for them, and re-layouts  2.69 us (2%)
    pallas_call x1, Pallas kernels, run_window(): pl.pallas_call(window, out_shape=(f32(*row), f32(*row), f32(*row), f32(*r...  137 us
    pallas_call x1, Pallas kernels, run_deliver(): pl.pallas_call(deliver, out_shape=tuple((jax.ShapeDtypeStruct(shape, F32)...  4.93 us

profile of v2, /device:TPU:2, one launch (start us, length us, event | category | flops | bytes accessed | tf_op | source)
XLA Modules:
  0.0 145.4 jit_solution(6842944242885683280)
XLA Ops:
  0.6 1.3 copy.26.evict
  2.0 1.3 copy.25.recall
  3.3 137.0 %shard_map.162 = (f32[128,1024]{1,0:T(8,128)}, f32[128,1024]{1,0:T(8,128)}, f32[128,1024]{1,0:T(8,128)}, f32[128,1024]{1,0:T(8,128)}, f32[128,1024]{1,0:T(8,128)...) custom-call(s32[8,2]{1,0:T(8,128)} %copy.26.evict, s32[8,2]{1,0:T(8,128)} %copy.25.recall, ...), custom_call_target="tpu_custom_call" | custom-call | tf_op jit(solution)/shard_map/pallas_call | solution.py:668
  140.3 4.9 %shard_map.163 = (f32[128,1024]{1,0:T(8,128)}, f32[128,1024]{1,0:T(8,128)}, f32[3,128,1024]{2,1,0:T(8,128)}, f32[3,128,1024]{2,1,0:T(8,128)}, f32[32,2048]{1,0:T...) custom-call(s32[8,2]{1,0:T(8,128)} %copy.26.evict, f32[3,128,1024]{2,1,0:T(8,128)} %bitcast.23, ...), custom_call_target="tpu_custom_call" | custom-call | tf_op jit(solution)/shard_map/pallas_call | solution.py:732

commit v3 on v2

--- a/solution.py
+++ b/solution.py
@@ -17,6 +17,7 @@
 RING = (2, 1, 3, 0)
 SIDES = ((0, 1, 3), (1, 3, 1))
 RB = 64
+LEFT = 1024
 
 
 def split(v):
@@ -46,7 +47,7 @@
 
 
 def window(
-    evict, recall, arriving, entering, returning, loss, kept, lent, w_in, taps, w_out,
+    slots, arriving, entering, returning, loss, kept, lent, w_in, taps, w_out,
     passed, returned, a1_out, x0_out, x1_out, g_in, g_tap, g_out,
     W, Wh, Wl, S, R1, R2, T1, T2, H, Xh, Xl, XN, XTh, XTl, ZTh, ZTl, DHh, DHl, Gh, Gl,
     U0, U1, DC, C, ZN, INV, DZ, ST, YR, DR, V0, V1, X0, X1, A, B, EDGE, PB, QB, TP, DT, TR,
@@ -201,7 +202,7 @@
     theirs = 7 - z
 
     def lent_slot(t):
-        return S[pl.ds(4 * jnp.clip(recall[theirs, t] - 3, 0, 2), 4), :, D : 2 * D].reshape(F, D)
+        return S[pl.ds(4 * jnp.clip(slots[4 * theirs + 2 + t] - 3, 0, 2), 4), :, D : 2 * D].reshape(F, D)
 
     @pl.when(z < 4)
     def _():
@@ -269,7 +270,7 @@
 
     @pl.when(z >= 4)
     def _():
-        ST[...] = S[pl.ds(4 * jnp.clip(recall[z, 0], 0, 2), 4), :, 0:D].reshape(F, D)
+        ST[...] = S[pl.ds(4 * jnp.clip(slots[4 * z + 2], 0, 2), 4), :, 0:D].reshape(F, D)
 
     norm_in(ST, 0)
     first_in.four(order[3:])
@@ -277,23 +278,25 @@
     first_in.five(order)
     first_out.three(order[:1])
 
-    def project(ah, al, row0, m, col0, n, out, unroll=2):
+    def project(ah, al, row0, m, col0, n, out, start=0, unroll=2):
         def body(j):
+            j = pl.multiple_of(start + j, 256)
             cols = pl.ds(pl.multiple_of(col0 + j, 256), 256)
             out[0:m, pl.ds(j, 256)] = dot3(
                 ah[row0 : row0 + m, :], al[row0 : row0 + m, :], Wh[:, cols], Wl[:, cols], NN
             )
 
-        loop(n, 256, body, unroll)
-
-    def project_back(ah, al, row0, col0, k, out, unroll=2):
+        loop(n - start, 256, body, unroll)
+
+    def project_back(ah, al, row0, col0, k, out, start=0, stop=D, unroll=2):
         def body(j):
+            j = pl.multiple_of(start + j, 256)
             out[:, pl.ds(j, 256)] = dot3(
                 ah[row0 : row0 + F, :], al[row0 : row0 + F, :],
                 Wh[pl.ds(j, 256), col0 : col0 + k], Wl[pl.ds(j, 256), col0 : col0 + k], NT,
             )
 
-        loop(D, 256, body, unroll)
+        loop(stop - start, 256, body, unroll)
 
     def gate_and_mix(row0, u_pad):
         def body(j, carry):
@@ -409,9 +412,9 @@
     def _():
         copy_x1.wait_recv()
 
-    use_own = (recall[z, 1] == evict[z, 0]).astype(jnp.int32)
-    use_lent = (recall[z, 1] >= 3).astype(jnp.int32)
-    slot1 = 4 * jnp.clip(recall[z, 1], 0, 2)
+    use_own = (slots[4 * z + 3] == slots[4 * z]).astype(jnp.int32)
+    use_lent = (slots[4 * z + 3] >= 3).astype(jnp.int32)
+    slot1 = 4 * jnp.clip(slots[4 * z + 3], 0, 2)
 
     def choose(r):
         own = jnp.broadcast_to(use_own, (32, D)) > 0
@@ -478,17 +481,17 @@
     def grad_out(j):
         weight_grad(ZTh, ZTl, Gh, Gl, pl.ds(j, 256), pl.ds(pl.multiple_of(IN + j, 256), 256))
 
-    def grad_in(base):
+    def grad_in(start, stop):
         def body(j):
-            cols = pl.ds(pl.multiple_of(base + j, 256), 256)
+            cols = pl.ds(pl.multiple_of(start + j, 256), 256)
             weight_grad(XTh, XTl, DHh, DHl, cols, cols)
 
-        loop(D, 256, body)
+        loop(stop - start, 256, body)
 
     class Reduce:
-        def __init__(self, col0, out, out0):
-            self.cols = slice(col0, col0 + D)
-            self.out, self.out_cols = out, slice(out0, out0 + D)
+        def __init__(self, col0, width, out, out0):
+            self.cols = slice(col0, col0 + width)
+            self.out, self.out_cols = out, slice(out0, out0 + width)
             self.pair, self.m1, self.m2, self.t1, self.t2 = {}, {}, {}, {}, {}
 
         def start(self):
@@ -570,30 +573,38 @@
                     total = total + T2[h, side, :, self.cols]
                 self.out[rows, self.out_cols] = total * SCALE
 
-    sum_out, sum_left, sum_right = Reduce(IN, g_out, 0), Reduce(0, g_in, 0), Reduce(D, g_in, D)
+    sum_out, sum_left = Reduce(IN, OUT, g_out, 0), Reduce(0, LEFT, g_in, 0)
+    sum_right = Reduce(LEFT, IN - LEFT, g_in, LEFT)
+    half = LEFT // 2
     loop(OUT, 256, grad_out)
     pl.semaphore_wait(free, 1)
     sum_out.start()
     project_back(Gh, Gl, F, IN, OUT, DZ)
+    unswish()
     sum_out.pairs()
-    unswish()
     unmix(1, U1)
-    sum_out.middle()
-    grad_in(0)
-    sum_left.start()
     tap_grads(1, U1)
     tap_round()
-    grad_in(D)
+    grad_in(0, half)
+    tap_round()
+    sum_out.middle()
+    grad_in(half, LEFT)
+    sum_left.start()
+    tap_round()
+    grad_in(LEFT, LEFT + 512)
+    sum_left.pairs()
+    grad_in(LEFT + 512, IN)
     sum_right.start()
-    sum_left.pairs()
+    sum_out.turn()
     tap_round()
-    sum_out.turn()
+    sum_right.pairs()
     sum_left.middle()
-    sum_right.pairs()
-    project_back(DHh, DHl, F, 0, IN, DZ)
-    tap_round()
+    project_back(DHh, DHl, F, 0, IN, DZ, 0, 512)
     sum_out.last()
     sum_right.middle()
+    project_back(DHh, DHl, F, 0, IN, DZ, 512, D)
+    tap_round()
+    sum_left.turn()
     input_cotangent(DR, QB)
     put_q = fetch(0, QB, returned)
 
@@ -610,23 +621,21 @@
 
     put_a = fetch(1, YR, a1_out)
     norm_in(YR, 0)
+    project(Xh, Xl, 0, F, 0, IN - 1024, H)
+    sum_left.last()
+    sum_out.finish()
+    project(Xh, Xl, 0, F, 0, IN, H, 1024)
+    gate_and_mix(0, U0)
+    sum_right.turn()
+    swish(False, True)
     tap_round()
-    sum_out.finish()
-    sum_left.turn()
-    project(Xh, Xl, 0, F, 0, IN, H)
-    sum_left.last()
-    tap_round()
-    gate_and_mix(0, U0)
-    swish(False, True)
     project(Xh, Xl, 0, F, IN, OUT, DZ)
+    sum_right.last()
     add_rows(YR, DZ, PB)
     put_p = fetch(2, PB, passed)
     put_x0 = fetch(3, X0, x0_out)
-    tap_round()
     g_tap[...] = DT[5, 0 : 8 * KW, :] * SCALE
-    sum_right.turn()
     sum_left.finish()
-    sum_right.last()
 
     @pl.when(z >= 4)
     def _():
@@ -670,7 +679,7 @@
         out_shape=(
             f32(*row), f32(*row), f32(*row), f32(*row), f32(*row), f32(32, IN), f32(8 * KW, 128), f32(32, OUT),
         ),
-        in_specs=[smem] * 2 + [hbm] * 7 + [vmem, hbm],
+        in_specs=[smem] + [hbm] * 7 + [vmem, hbm],
         out_specs=(hbm,) * 5 + (vmem,) * 3,
         scratch_shapes=scratch,
         compiler_params=pltpu.CompilerParams(
@@ -680,7 +689,7 @@
 
 
 def deliver(
-    evict, kept, lent, arriving, a1, x0, x1, passed, returned, g_in, g_tap, g_out,
+    slots, kept, lent, arriving, a1, x0, x1, passed, returned, g_in, g_tap, g_out,
     o_passed, o_returned, o_kept, o_lent, o_in, o_tap, o_out,
     v_passed, v_returned, v_kept, v_lent, v_in, v_tap, v_out, sems,
 ):
@@ -699,8 +708,8 @@
         (7 - z, 3, lent, v_lent, o_lent, x0, x1),
     ):
         for i in range(3):
-            is_early = evict[section, 0] == base + i
-            is_late = evict[section, 1] == base + i
+            is_early = slots[4 * section] == base + i
+            is_late = slots[4 * section + 1] == base + i
             sem = sems.at[0, len(moves)]
 
             @pl.when(is_late)
@@ -742,13 +751,14 @@
     arriving, entering, returning, loss_grad, kept, lent, w_in, kernel, w_out, evict, recall
 ):
     arrived = arriving[0, 0]
+    slots = jnp.concatenate([evict, recall], axis=1).reshape(32)
     kept_now, lent_now = kept[0, :, 0], lent[0, :, 0]
     passed, returned, a1, x0, x1, g_in, g_tap, g_out = run_window(
-        evict, recall, arrived, entering[0, 0], returning[0, 0], loss_grad[0, 0],
+        slots, arrived, entering[0, 0], returning[0, 0], loss_grad[0, 0],
         kept_now.reshape(12, 32, D), lent_now.reshape(12, 32, D), w_in[0], kernel.reshape(8 * KW, 128), w_out[0],
     )
     passed, returned, kept_out, lent_out, g_in, g_tap, g_out = run_deliver(
-        evict, kept_now, lent_now, arrived, a1, x0, x1, passed, returned, g_in, g_tap, g_out
+        slots, kept_now, lent_now, arrived, a1, x0, x1, passed, returned, g_in, g_tap, g_out
     )
     return (
         passed[None, None], returned[None, None], kept_out[None, :, None], lent_out[None, :, None],

time: 146 us -> 147 us (level); the launches traced: 145 us -> 145 us
  local copies, waits for them, and re-layouts: 2.69 us -> 0.76 us
    unnamed x2 -> x0, local copies, waits for them, and re-layouts: 2.69 us -> none
where the time goes in v3:
time: 147 us; the launch traced here: 145 us
  Pallas kernels  142 us (97%)
    pallas_call x1, Pallas kernels, run_window(): pl.pallas_call(window, out_shape=(f32(*row), f32(*row), f32(*row), f32(*r...  137 us
    pallas_call x1, Pallas kernels, run_deliver(): pl.pallas_call(deliver, out_shape=tuple((jax.ShapeDtypeStruct(shape, F32)...  4.87 us

profile of v3, /device:TPU:2, one launch (start us, length us, event | category | flops | bytes accessed | tf_op | source)
XLA Modules:
  0.0 144.5 jit_solution(1213346092772417949)
XLA Ops:
  0.6 0.7 pad_add_fusion
  1.3 0.1 copy.22
  1.4 0.7 reshape.23.slots
  2.1 137.4 %shard_map.162 = (f32[128,1024]{1,0:T(8,128)}, f32[128,1024]{1,0:T(8,128)}, f32[128,1024]{1,0:T(8,128)}, f32[128,1024]{1,0:T(8,128)}, f32[128,1024]{1,0:T(8,128)...) custom-call(s32[32]{0:T(128)} %reshape.23.slots, f32[128,1024]{1,0:T(8,128)} %bitcast.26, ...), custom_call_target="tpu_custom_call" | custom-call | tf_op jit(solution)/shard_map/pallas_call | solution.py:677
  139.5 4.9 %shard_map.163 = (f32[128,1024]{1,0:T(8,128)}, f32[128,1024]{1,0:T(8,128)}, f32[3,128,1024]{2,1,0:T(8,128)}, f32[3,128,1024]{2,1,0:T(8,128)}, f32[32,2048]{1,0:T...) custom-call(s32[32]{0:T(128)} %reshape.23.slots, f32[3,128,1024]{2,1,0:T(8,128)} %bitcast.23, f32[3,128,1024]{2,1,0:T(8,128)} %bitcast.25, ...), custom_call_target="tpu_custom_call" | custom-call | tf_op jit(solution)/shard_map/pallas_call | solution.py:741
